TPU v7x, 32 devices: a whole 2x2x4 slice. The times are simulated.
32 devices in a mesh: gx: 8 (over z, core), gy: 4 (over y, x).
Axes of the slice: x: 2, y: 2, z: 4, core: 2. Of those that a mesh axis runs over, the one named last changes fastest.
Arguments:
- source: float32 [2, 256, 1024], P(None, 'gx', 'gy'), may hold values from -8 to 8
- coef_x: float32 [2, 256, 1024], P(None, 'gx', 'gy'), may hold values from 0.2 to 5
- coef_y: float32 [2, 256, 1024], P(None, 'gx', 'gy'), may hold values from 0.2 to 5
- coef_z: float32 [256, 1024], P('gx', 'gy'), may hold values from 1 to 20
- surface: float32 [2, 256, 1024], P(None, 'gx', 'gy'), may hold values from 0.05 to 0.5
Outputs:
- pressure: float32 [2, 256, 1024], P(None, 'gx', 'gy')
- residual: float32 [2, 256, 1024], P(None, 'gx', 'gy')
All inputs are finite; a program needn't handle non-finite values.
Results may differ from a plain program's by a relative error of at most 0.0003.
Values sent between devices are 32-bit elements; how exact they have to be, the bound alone decides.
No kernel may reach another device: no remote copies, remote signals or barrier semaphores. Data moves between devices by JAX's collectives and lax.ppermute only.
A program may use at most 64 MiB of HBM per device.

v0:
```python
import jax
import jax.numpy as jnp
from jax import lax
from jax.sharding import PartitionSpec as P

LEVELS = 4
PRE = 2
POST = 2
CSWEEPS = 8


damping = 0.8


def extended(block, sides, width):
    for axis, dim in sides:
        count = lax.axis_size(axis)
        forward = [(i, i + 1) for i in range(count - 1)]
        backward = [(target, source) for source, target in forward]
        low = lax.ppermute(
            lax.slice_in_dim(block, block.shape[dim] - width, None, axis=dim), axis, forward
        )
        high = lax.ppermute(lax.slice_in_dim(block, 0, width, axis=dim), axis, backward)
        block = jnp.concatenate([low, block, high], axis=dim)
    return block


def passed_along(shard, axis, by):
    length = lax.axis_size(axis)
    pairs = [(i, i + by) for i in range(length) if 0 <= i + by < length]
    return lax.ppermute(shard, axis, pairs)


def operate(u_ext, kx_ext, ky_ext, kz, surf):
    u = u_ext[:, 1:-1, 1:-1]
    kx_hi = kx_ext[:, 1:, :]
    kx_lo = kx_ext[:, :-1, :]
    ky_hi = ky_ext[:, :, 1:]
    ky_lo = ky_ext[:, :, :-1]
    vert = kz * (u[0] - u[1])
    result = surf * u + kx_hi * (u - u_ext[:, 2:, 1:-1]) + kx_lo * (u - u_ext[:, :-2, 1:-1])
    result = result + ky_hi * (u - u_ext[:, 1:-1, 2:]) + ky_lo * (u - u_ext[:, 1:-1, :-2])
    return result + jnp.stack([vert, -vert])


def diagonal(kx_ext, ky_ext, kz, surf):
    return (
        surf
        + kx_ext[:, 1:, :]
        + kx_ext[:, :-1, :]
        + ky_ext[:, :, 1:]
        + ky_ext[:, :, :-1]
        + kz[None]
    )


def coarsen(kx, ky, kz, surf):
    kx_c = kx[:, 1::2, 0::2] + kx[:, 1::2, 1::2]
    ky_c = ky[:, 0::2, 1::2] + ky[:, 1::2, 1::2]
    kz_c = kz[0::2, 0::2] + kz[1::2, 0::2] + kz[0::2, 1::2] + kz[1::2, 1::2]
    s_c = surf[:, 0::2, 0::2] + surf[:, 1::2, 0::2] + surf[:, 0::2, 1::2] + surf[:, 1::2, 1::2]
    return (kx_c, ky_c, kz_c, s_c)


def restrict(field):
    return field[:, 0::2, 0::2] + field[:, 1::2, 0::2] + field[:, 0::2, 1::2] + field[:, 1::2, 1::2]


def prolong(field):
    return jnp.repeat(jnp.repeat(field, 2, axis=1), 2, axis=2)


def extend(u):
    return extended(u, (("gx", 1), ("gy", 2)), 1)


def extend_final(u):
    return extended(u, (("gx", 1), ("gy", 2)), 1)


def pad_global(u):
    return jnp.pad(u, ((0, 0), (1, 1), (1, 1)))


def sweeps(level, rhs_now, count, widen):
    kx_ext, ky_ext, kz, surf = level
    diag = diagonal(kx_ext, ky_ext, kz, surf)
    u = damping * rhs_now / diag
    for step in range(count - 1):
        u = u + damping * (rhs_now - operate(widen(u), kx_ext, ky_ext, kz, surf)) / diag
    return (u, diag)


def assemble_layers(stacked, rows_dev, cols_dev):
    count_x = lax.axis_size("gx")
    count_y = lax.axis_size("gy")
    blocks = stacked.reshape(count_x, count_y, stacked.shape[1], rows_dev, cols_dev)
    blocks = jnp.transpose(blocks, (2, 0, 3, 1, 4))
    return blocks.reshape(stacked.shape[1], count_x * rows_dev, count_y * cols_dev)


def assemble_plane(stacked, rows_dev, cols_dev):
    count_x = lax.axis_size("gx")
    count_y = lax.axis_size("gy")
    blocks = stacked.reshape(count_x, count_y, rows_dev, cols_dev)
    blocks = jnp.transpose(blocks, (0, 2, 1, 3))
    return blocks.reshape(count_x * rows_dev, count_y * cols_dev)


def coarse_solve(coarse_level, rhs_now):
    kx_ext, ky_ext, kz, surf = coarse_level
    rows_dev = rhs_now.shape[1]
    cols_dev = rhs_now.shape[2]
    kx_own = kx_ext[:, 1:, :]
    ky_own = ky_ext[:, :, 1:]
    pieces = (
        lax.all_gather(rhs_now[None], ("gx", "gy"), axis=0, tiled=True),
        lax.all_gather(kx_own[None], ("gx", "gy"), axis=0, tiled=True),
        lax.all_gather(ky_own[None], ("gx", "gy"), axis=0, tiled=True),
        lax.all_gather(kz[None], ("gx", "gy"), axis=0, tiled=True),
        lax.all_gather(surf[None], ("gx", "gy"), axis=0, tiled=True),
    )
    rhs_all = assemble_layers(pieces[0], rows_dev, cols_dev)
    kx_all = assemble_layers(pieces[1], rows_dev, cols_dev)
    ky_all = assemble_layers(pieces[2], rows_dev, cols_dev)
    kz_all = assemble_plane(pieces[3], rows_dev, cols_dev)
    surf_all = assemble_layers(pieces[4], rows_dev, cols_dev)
    kx_pad = jnp.pad(kx_all, ((0, 0), (1, 0), (0, 0)))
    ky_pad = jnp.pad(ky_all, ((0, 0), (0, 0), (1, 0)))
    whole, unused = sweeps((kx_pad, ky_pad, kz_all, surf_all), rhs_all, CSWEEPS, pad_global)
    whole_resid = rhs_all - operate(pad_global(whole), kx_pad, ky_pad, kz_all, surf_all)
    offset = jnp.sum(whole_resid) / jnp.sum(surf_all)
    start_x = lax.axis_index("gx") * rows_dev
    start_y = lax.axis_index("gy") * cols_dev
    zero = jnp.zeros((), jnp.int32)
    mine = lax.dynamic_slice(whole, (zero, start_x, start_y), (whole.shape[0], rows_dev, cols_dev))
    return mine + offset


def cycle(levels, wides, depth, rhs_now):
    if depth == LEVELS:
        return coarse_solve(levels[depth], rhs_now)
    kx_ext, ky_ext, kz, surf = levels[depth]
    u, diag = sweeps(levels[depth], rhs_now, PRE, extend)
    resid = rhs_now - operate(extend(u), kx_ext, ky_ext, kz, surf)
    u = u + prolong(cycle(levels, wides, depth + 1, restrict(resid)))
    for step in range(POST):
        u = u + damping * (rhs_now - operate(extend(u), kx_ext, ky_ext, kz, surf)) / diag
    return u


def on_device(source, coef_x, coef_y, coef_z, surface):
    rows_dev = source.shape[1]
    cols_dev = source.shape[2]
    row_index = lax.axis_index("gx") * rows_dev + lax.broadcasted_iota(
        jnp.int32, (1, rows_dev, 1), 1
    )
    col_index = lax.axis_index("gy") * cols_dev + lax.broadcasted_iota(
        jnp.int32, (1, 1, cols_dev), 2
    )
    kx = jnp.where(row_index == lax.axis_size("gx") * rows_dev - 1, jnp.float32(0.0), coef_x)
    ky = jnp.where(col_index == lax.axis_size("gy") * cols_dev - 1, jnp.float32(0.0), coef_y)
    kz, surf = (coef_z, surface)
    rim_x = passed_along(kx[:, -1:, :], "gx", 1)
    rim_y = passed_along(ky[:, :, -1:], "gy", 1)
    levels = []
    wides = []
    for depth in range(LEVELS + 1):
        levels.append(
            (jnp.concatenate([rim_x, kx], axis=1), jnp.concatenate([rim_y, ky], axis=2), kz, surf)
        )
        if depth < LEVELS:
            kx, ky, kz, surf = coarsen(kx, ky, kz, surf)
            rim_x = rim_x[:, :, 0::2] + rim_x[:, :, 1::2]
            rim_y = rim_y[:, 0::2, :] + rim_y[:, 1::2, :]
    pressure = cycle(levels, wides, 0, source)
    kx_ext, ky_ext, kz, surf = levels[0]
    residual = source - operate(extend_final(pressure), kx_ext, ky_ext, kz, surf)
    return (pressure, residual)


def solution(mesh):
    in_specs = (
        P(None, "gx", "gy"),
        P(None, "gx", "gy"),
        P(None, "gx", "gy"),
        P("gx", "gy"),
        P(None, "gx", "gy"),
    )
    out_specs = (P(None, "gx", "gy"), P(None, "gx", "gy"))
    return jax.shard_map(
        on_device, mesh=mesh, in_specs=in_specs, out_specs=out_specs, check_vma=False
    )
```

profile of v0, /device:TPU:0, one launch (start us, length us, event | category | flops | bytes accessed | tf_op | source)
XLA Modules:
  0.0 601.6 jit_solution(8879207958817343261)
XLA Ops:
  1.6 4.8 collective-permute-start.1
  13.1 66.3 %all-gather.3 = f32[64,2,16]{2,1,0:T(2,128)S(1)} all-gather(f32[2,2,16]{2,1,0:T(2,128)S(1)} %add.870), channel_id=5, replica_groups=mesh['gx'=8,'gy'=4] {'gx','gy'}, dimensions={0}, use_global_device_ids=true | all-gather | bytes 8448 | tf_op jit(solution)/shard_map/all_gather | solution.py:119
  83.0 3.0 collective-permute-start.3
  86.0 63.7 %all-gather.2 = f32[64,2,16]{2,1,0:T(2,128)S(1)} all-gather(f32[2,2,16]{2,1,0:T(2,128)S(1)} %add.867), channel_id=4, replica_groups=mesh['gx'=8,'gy'=4] {'gx','gy'}, dimensions={0}, use_global_device_ids=true | all-gather | bytes 8448 | tf_op jit(solution)/shard_map/all_gather | solution.py:118
  152.3 4.2 collective-permute-start.5
  158.1 4.2 collective-permute-done.4
  163.8 3.0 collective-permute-start.7
  166.9 64.3 %all-gather.5 = f32[32,2,16]{2,1,0:T(2,128)S(1)} all-gather(f32[1,2,16]{2,1,0:T(2,128)S(1)} %add_bitcast_fusion), channel_id=6, replica_groups=mesh['gx'=8,'gy'=4] {'gx','gy'}, dimensions={0}, use_global_device_ids=true | all-gather | bytes 4224 | tf_op jit(solution)/shard_map/all_gather | solution.py:120
  231.8 3.3 collective-permute-start.9
  236.7 4.2 collective-permute-done.8
  245.0 3.0 collective-permute-start.11
  253.2 4.2 collective-permute-done.12
  267.9 4.2 collective-permute-done.16
  274.4 3.0 collective-permute-start.19
  282.6 4.2 collective-permute-done.20
  288.2 3.6 collective-permute-start.23
  292.7 3.1 collective-permute-start.25
  297.3 4.2 collective-permute-done.24
  303.9 4.4 collective-permute-start.27
  308.3 64.8 %all-gather.1 = f32[64,2,16]{2,1,0:T(2,128)S(1)} all-gather(f32[2,2,16]{2,1,0:T(2,128)S(1)} %add_add_fusion.10), channel_id=3, replica_groups=mesh['gx'=8,'gy'=4] {'gx','gy'}, dimensions={0}, use_global_device_ids=true | all-gather | bytes 8448 | tf_op jit(solution)/shard_map/all_gather | solution.py:121
  378.4 4.2 collective-permute-done.28
  392.1 4.2 collective-permute-done.32
  396.8 64.5 %all-gather = f32[64,2,16]{2,1,0:T(2,128)S(1)} all-gather(f32[2,2,16]{2,1,0:T(2,128)S(1)} %add_add_fusion.11), channel_id=2, replica_groups=mesh['gx'=8,'gy'=4] {'gx','gy'}, dimensions={0}, use_global_device_ids=true | all-gather | bytes 8448 | tf_op jit(solution)/shard_map/all_gather | solution.py:117
  465.9 3.0 collective-permute-start.35
  469.9 3.3 collective-permute-start.37
  474.5 4.2 collective-permute-done.36
  480.1 3.0 collective-permute-start.39
  488.2 4.2 collective-permute-done.40
  494.0 3.0 collective-permute-start.43
  502.2 4.2 collective-permute-done.44
  507.8 4.4 collective-permute-start.47
  513.1 3.1 collective-permute-start.49
  517.6 4.2 collective-permute-done.48
  523.4 4.4 collective-permute-start.51
  528.7 3.1 collective-permute-start.53
  533.3 4.2 collective-permute-done.52
  539.0 4.4 collective-permute-start.55
  544.3 3.1 collective-permute-start.57
  548.9 4.2 collective-permute-done.56
  554.9 4.4 collective-permute-start.59
  560.2 3.1 collective-permute-start.61
  565.0 4.2 collective-permute-done.60
  570.7 4.4 collective-permute-start.63
  576.0 3.1 collective-permute-start.65
  580.8 4.2 collective-permute-done.64
  586.5 4.4 collective-permute-start.67
  591.8 3.1 collective-permute-start.69
  596.6 4.2 collective-permute-done.68
  (348 shorter events, 109.9 us)
Async XLA Ops:
  1.6 80.0 %collective-permute-start.1 = (f32[2,32,1]{2,1,0:T(8,128)S(1)}, f32[2,32,1]{2,1,0:T(8,128)S(1)}, u32[]{:S(2)}, u32[]{:S(2)}) collective-permute-start(f32[2,32,1]{2,1,0:T(8,128)S(1)} %slice.1369), channel_id=1, source_target_pairs={{0,1},{1,2},{2,3},{4,5},{5,6},{6,7},{8,9},{9,10},{10,11},{12,13},{... | collective-permute-start | bytes 776 | tf_op jit(solution)/shard_map/ppermute | solution.py:31
  6.5 75.0 %collective-permute-start = (f32[2,1,256]{2,1,0:T(1,128)S(1)}, f32[2,1,256]{2,1,0:T(1,128)S(1)}, u32[]{:S(2)}, u32[]{:S(2)}) collective-permute-start(f32[2,1,256]{2,1,0:T(1,128)S(1)} %slice.1368), channel_id=1, source_target_pairs={{0,4},{4,8},{8,12},{12,16},{16,20},{20,24},{24,28},{1,5},{5,9},{9,... | collective-permute-start | bytes 6152 | tf_op jit(solution)/shard_map/ppermute | solution.py:31
  81.7 70.5 %collective-permute-start.2 = (f32[2,1,256]{2,1,0:T(1,128)S(1)}, f32[2,1,256]{2,1,0:T(1,128)S(1)}, u32[]{:S(2)}, u32[]{:S(2)}) collective-permute-start(f32[2,1,256]{2,1,0:T(1,128)S(1)} %get-tuple-element.56), channel_id=1, source_target_pairs={{4,0},{8,4},{12,8},{16,12},{20,16},{24,20},{28,24},{5,1},{9,5},{13... | collective-permute-start | bytes 6152 | tf_op jit(solution)/shard_map/ppermute | solution.py:23
  83.0 69.2 %collective-permute-start.3 = (f32[2,1,256]{2,1,0:T(1,128)S(1)}, f32[2,1,256]{2,1,0:T(1,128)S(1)}, u32[]{:S(2)}, u32[]{:S(2)}) collective-permute-start(f32[2,1,256]{2,1,0:T(1,128)S(1)} %get-tuple-element.55), channel_id=1, source_target_pairs={{0,4},{4,8},{8,12},{12,16},{16,20},{20,24},{24,28},{1,5},{5,9},{9,... | collective-permute-start | bytes 6152 | tf_op jit(solution)/shard_map/ppermute | solution.py:20
  152.3 5.8 collective-permute-start.5
  156.5 5.9 collective-permute-start.4
  162.5 69.1 %collective-permute-start.6 = (f32[2,1,256]{2,1,0:T(1,128)S(1)}, f32[2,1,256]{2,1,0:T(1,128)S(1)}, u32[]{:S(2)}, u32[]{:S(2)}) collective-permute-start(f32[2,1,256]{2,1,0:T(1,128)S(1)} %get-tuple-element.54), channel_id=1, source_target_pairs={{4,0},{8,4},{12,8},{16,12},{20,16},{24,20},{28,24},{5,1},{9,5},{13... | collective-permute-start | bytes 6152 | tf_op jit(solution)/shard_map/ppermute | solution.py:23
  163.8 67.8 %collective-permute-start.7 = (f32[2,1,256]{2,1,0:T(1,128)S(1)}, f32[2,1,256]{2,1,0:T(1,128)S(1)}, u32[]{:S(2)}, u32[]{:S(2)}) collective-permute-start(f32[2,1,256]{2,1,0:T(1,128)S(1)} %get-tuple-element.53), channel_id=1, source_target_pairs={{0,4},{4,8},{8,12},{12,16},{16,20},{20,24},{24,28},{1,5},{5,9},{9,... | collective-permute-start | bytes 6152 | tf_op jit(solution)/shard_map/ppermute | solution.py:20
  231.8 5.0 collective-permute-start.9
  235.1 5.9 collective-permute-start.8
  243.7 4.7 collective-permute-start.10
  251.7 5.7 collective-permute-start.12
  257.6 5.9 collective-permute-start.14
  266.4 5.7 collective-permute-start.16
  273.1 4.8 collective-permute-start.18
  281.2 5.6 collective-permute-start.20
  286.9 4.9 collective-permute-start.22
  295.8 5.6 collective-permute-start.24
  302.6 71.3 %collective-permute-start.26 = (f32[2,1,32]{2,1,0:T(1,128)S(1)}, f32[2,1,32]{2,1,0:T(1,128)S(1)}, u32[]{:S(2)}, u32[]{:S(2)}) collective-permute-start(f32[2,1,32]{2,1,0:T(1,128)S(1)} %get-tuple-element.128), channel_id=1, source_target_pairs={{4,0},{8,4},{12,8},{16,12},{20,16},{24,20},{28,24},{5,1},{9,5},{13... | collective-permute-start | bytes 776 | tf_op jit(solution)/shard_map/ppermute | solution.py:23
  303.9 70.1 %collective-permute-start.27 = (f32[2,1,32]{2,1,0:T(1,128)S(1)}, f32[2,1,32]{2,1,0:T(1,128)S(1)}, u32[]{:S(2)}, u32[]{:S(2)}) collective-permute-start(f32[2,1,32]{2,1,0:T(1,128)S(1)} %get-tuple-element.127), channel_id=1, source_target_pairs={{0,4},{4,8},{8,12},{12,16},{16,20},{20,24},{24,28},{1,5},{5,9},{9,... | collective-permute-start | bytes 776 | tf_op jit(solution)/shard_map/ppermute | solution.py:20
  377.0 5.5 collective-permute-start.28
  390.7 5.5 collective-permute-start.32
  469.9 4.7 collective-permute-start.37
  473.2 5.5 collective-permute-start.36
  486.9 5.5 collective-permute-start.40
  500.8 5.6 collective-permute-start.44
  506.5 5.7 collective-permute-start.46
  507.8 5.2 collective-permute-start.47
  516.2 5.6 collective-permute-start.48
  522.1 5.7 collective-permute-start.50
  523.4 5.2 collective-permute-start.51
  528.7 4.6 collective-permute-start.53
  531.8 5.7 collective-permute-start.52
  537.7 5.7 collective-permute-start.54
  539.0 5.2 collective-permute-start.55
  547.4 5.7 collective-permute-start.56
  553.6 5.7 collective-permute-start.58
  554.9 5.2 collective-permute-start.59
  560.2 4.8 collective-permute-start.61
  563.3 5.9 collective-permute-start.60
  569.4 5.7 collective-permute-start.62
  570.7 5.2 collective-permute-start.63
  576.0 4.8 collective-permute-start.65
  579.1 5.9 collective-permute-start.64
  585.2 5.8 collective-permute-start.66
  586.5 5.3 collective-permute-start.67
  591.8 4.8 collective-permute-start.69
  594.9 5.9 collective-permute-start.68
  (27 other events, 118.2 us)
where the time goes:
time: 606 us; the launch traced here: 602 us
  blocking collectives  324 us (53%)
  starting transfers between devices  165 us (27%)
  waiting for transfers between devices  84 us (14%)
  local copies, waits for them, and re-layouts  19.5 us (3%)
  other arithmetic  6.51 us (1%)
    ppermute x34, starting transfers between devices, extended(): lax.ppermute(lax.slice_in_dim(block, block.shape[dim] - width, None, axis...  114 us
    ppermute x34, waiting for transfers between devices, extended(): lax.ppermute(lax.slice_in_dim(block, 0, width, axis=dim), axis, backward)  71.7 us
    all_gather x1, blocking collectives, coarse_solve(): lax.all_gather(ky_own[None], ('gx', 'gy'), axis=0, tiled=True)  66.3 us
    all_gather x1, blocking collectives, coarse_solve(): lax.all_gather(surf[None], ('gx', 'gy'), axis=0, tiled=True)  64.8 us
    all_gather x1, blocking collectives, coarse_solve(): lax.all_gather(rhs_now[None], ('gx', 'gy'), axis=0, tiled=True)  64.5 us
    all_gather x1, blocking collectives, coarse_solve(): lax.all_gather(kz[None], ('gx', 'gy'), axis=0, tiled=True)  64.3 us
    all_gather x1, blocking collectives, coarse_solve(): lax.all_gather(kx_own[None], ('gx', 'gy'), axis=0, tiled=True)  63.7 us
    ppermute x34, starting transfers between devices, extended(): lax.ppermute(lax.slice_in_dim(block, 0, width, axis=dim), axis, backward)  44.1 us
  transfers between devices with their start and end apart: 70, of which 42 were waited for; matrix products, arithmetic and copies ran while one was open for 2% of the time, Pallas kernels for 0%

commit v1 on v0

v1 whole, which is shorter than its diff:
```python
import functools

import jax
import jax.numpy as jnp
from jax import lax
from jax.experimental import pallas as pl
from jax.experimental.pallas import tpu as pltpu
from jax.sharding import PartitionSpec as P

LEVELS = 4
PRE = 2
POST = 2
CSWEEPS = 8
damping = 0.8

LANES = 128
WIDTH = 28
PAD = 8
PLANES = 9
F, KX, KY, S, KZ = 0, 2, 4, 6, 8
W, U = 9, 11


def pair_permute(x, axis, first):
    count = lax.axis_size(axis)
    pairs = []
    for i in range(first, count - 1, 2):
        pairs += [(i, i + 1), (i + 1, i)]
    return lax.ppermute(x, axis, pairs)


def lane_iota(shape):
    return lax.broadcasted_iota(jnp.int32, shape, len(shape) - 1)


def from_right(x, step):
    rolled = pltpu.roll(x, LANES - step, x.ndim - 1)
    if x.shape[1] == 1:
        return rolled
    after = jnp.concatenate([rolled[:, 1:], rolled[:, :1]], axis=1)
    return jnp.where(lane_iota(x.shape) >= LANES - step, after, rolled)


def from_left(x, step):
    rolled = pltpu.roll(x, step, x.ndim - 1)
    if x.shape[1] == 1:
        return rolled
    before = jnp.concatenate([rolled[:, -1:], rolled[:, :-1]], axis=1)
    return jnp.where(lane_iota(x.shape) < step, before, rolled)


def weight(kx, kx_lo, ky, kz, surf, step):
    diag = surf + kx + kx_lo + ky + from_left(ky, step) + kz
    return jnp.where(diag > 0.0, damping / jnp.where(diag > 0.0, diag, 1.0), 0.0)


def residual_of(f, u, u_up, u_dn, kx, kx_lo, ky, kz, surf, step):
    flux = ky * (u - from_right(u, step))
    vert = kz * (u[0:1] - u[1:2])
    out = surf * u + kx * (u - u_up) + kx_lo * (u - u_dn)
    out = out + flux - from_left(flux, step)
    return f - (out + jnp.concatenate([vert, -vert], axis=0))


def rows_of(ref, plane, count, start, size=8):
    return ref[plane : plane + count, :, start : start + size, :]


def block_residual(level, u_ref, u_at, step, r0):
    u = rows_of(u_ref, u_at, 2, r0)
    return u, residual_of(
        rows_of(level, F, 2, r0),
        u,
        rows_of(u_ref, u_at, 2, r0 + 1),
        rows_of(u_ref, u_at, 2, r0 - 1),
        rows_of(level, KX, 2, r0),
        rows_of(level, KX, 2, r0 - 1),
        rows_of(level, KY, 2, r0),
        rows_of(level, KZ, 1, r0),
        rows_of(level, S, 2, r0),
        step,
    )


def put(ref, plane, r0, value):
    ref[plane : plane + value.shape[0], :, r0 : r0 + value.shape[2], :] = value


def strided(ref, plane, count, start, size):
    tiles = ref.shape[1]
    return jnp.stack(
        [
            jnp.stack([ref[plane + p, c, pl.ds(start, size, stride=2), :] for c in range(tiles)])
            for p in range(count)
        ]
    )


def put_strided(ref, plane, start, value):
    for p in range(value.shape[0]):
        for c in range(value.shape[1]):
            ref[plane + p, c, pl.ds(start, value.shape[2], stride=2), :] = value[p, c]


def zero_pads(ref, planes):
    rows = ref.shape[2]
    for plane in planes:
        zero = jnp.zeros((1, ref.shape[1], PAD, LANES), jnp.float32)
        put(ref, plane, 0, zero)
        put(ref, plane, rows - PAD, zero)


def coarse_block(fine, resid, step, fine_row, size):
    def both(ref, plane, count):
        return strided(ref, plane, count, fine_row, size) + strided(
            ref, plane, count, fine_row + 1, size
        )

    f = both(resid, 0, 2)
    kx = strided(fine, KX, 2, fine_row + 1, size)
    ky = both(fine, KY, 2)
    surf_kz = both(fine, S, 3)
    summed = jnp.concatenate([f, kx, surf_kz], axis=0)
    summed = summed + from_right(summed, step)
    return summed[0:2], summed[2:4], from_right(ky, step), summed[4:7]


def sides(mine, other, is_even):
    low = jnp.where(is_even, other, mine)
    high = jnp.where(is_even, mine, other)
    return low, high


def strip_kernel(own_ref, near_ref, far_ref, c_ref, d_ref):
    even_x = lax.rem(lax.axis_index("gx"), 2) == 0
    even_y = lax.rem(lax.axis_index("gy"), 2) == 0
    rows = own_ref.shape[1]
    cols = own_ref.shape[2]
    lane = lane_iota((8, LANES))

    def place(pieces, offset):
        tiles = [jnp.zeros((8, LANES), jnp.float32)] * 2
        for p in range(PLANES):
            begin = p * WIDTH
            rolled = pltpu.roll(pieces[p], (begin - offset) % LANES, 1)
            for a in range(2):
                lo, hi = begin - a * LANES, begin + WIDTH - a * LANES
                if hi > 0 and lo < LANES:
                    tiles[a] = jnp.where((lane >= lo) & (lane < hi), rolled, tiles[a])
        return tiles

    for block in range(3 * rows // 8):
        part, r0 = divmod(block * 8, rows)
        first, last = [], []
        for p in range(PLANES):
            for held, column in ((first, 0), (last, cols - LANES)):
                at = (p, slice(r0, r0 + 8), slice(column, column + LANES))
                if part == 1:
                    held.append(own_ref[at])
                else:
                    held.append(sides(near_ref[at], far_ref[at], even_x)[part // 2])
        left = place(first, 0)
        right = place(last, LANES - WIDTH)
        for a in range(2):
            at = (slice(block * 8, block * 8 + 8), slice(a * LANES, (a + 1) * LANES))
            c_ref[at] = jnp.where(even_y, right[a], left[a])
            d_ref[at] = jnp.where(even_y, left[a], right[a])


def down_kernel(own_ref, near_ref, far_ref, c_ref, d_ref, l0, l1, l2, pack_ref, ua, rr):
    even_x = lax.rem(lax.axis_index("gx"), 2) == 0
    even_y = lax.rem(lax.axis_index("gy"), 2) == 0
    rows = own_ref.shape[1]
    lane = lane_iota((8, LANES))

    def take(tiles, p, offset):
        begin = p * WIDTH
        a, b = begin // LANES, (begin + WIDTH - 1) // LANES
        piece = tiles[a]
        if a != b:
            piece = jnp.where(lane < begin + WIDTH - b * LANES, tiles[b], tiles[a])
        return pltpu.roll(piece, (offset - begin) % LANES, 1)

    for block in range(3 * rows // 8):
        part, r0 = divmod(block * 8, rows)
        to = slice(PAD + block * 8, PAD + block * 8 + 8)
        for p in range(PLANES):
            for c in range(2):
                at = (p, slice(r0, r0 + 8), slice(c * LANES, (c + 1) * LANES))
                if part == 1:
                    l0[p, c, to, :] = own_ref[at]
                else:
                    l0[p, c, to, :] = sides(near_ref[at], far_ref[at], even_x)[part // 2]
        low, high = [], []
        for a in range(2):
            at = (slice(block * 8, block * 8 + 8), slice(a * LANES, (a + 1) * LANES))
            lo, hi = sides(c_ref[at], d_ref[at], even_y)
            low.append(lo)
            high.append(hi)
        for p in range(PLANES):
            right = take(high, p, 0)
            left = take(low, p, LANES - WIDTH)
            l0[p, 2, to, :] = jnp.where(
                lane < WIDTH, right, jnp.where(lane >= LANES - WIDTH, left, 0.0)
            )

    for ref in (l0, l1, l2):
        zero_pads(ref, (KX, KX + 1, U, U + 1))
    for ref in (ua,):
        zero_pads(ref, (0, 1))

    levels = (l0, l1, l2)
    for depth, level in enumerate(levels):
        step = 1 << depth
        count = level.shape[2] - 2 * PAD
        starts = range(PAD, PAD + count, 8)
        if depth:
            for r0 in starts:
                f, kx, ky, surf_kz = coarse_block(
                    levels[depth - 1], rr, step // 2, PAD + 2 * (r0 - PAD), 8
                )
                put(level, F, r0, f)
                put(level, KX, r0, kx)
                put(level, KY, r0, ky)
                put(level, S, r0, surf_kz)
            if count * 2 + 2 * PAD > 0:
                put(ua, 0, PAD + count, jnp.zeros((2, 3, PAD, LANES), jnp.float32))
        for r0 in starts:
            w = weight(
                rows_of(level, KX, 2, r0),
                rows_of(level, KX, 2, r0 - 1),
                rows_of(level, KY, 2, r0),
                rows_of(level, KZ, 1, r0),
                rows_of(level, S, 2, r0),
                step,
            )
            put(level, W, r0, w)
            put(ua, 0, r0, w * rows_of(level, F, 2, r0))
        for r0 in starts:
            u, r = block_residual(level, ua, 0, step, r0)
            put(level, U, r0, u + rows_of(level, W, 2, r0) * r)
        for r0 in starts:
            put(rr, 0, r0, block_residual(level, level, U, step, r0)[1])

    own = l2.shape[2] // 2 - 4
    f, kx, ky, surf_kz = coarse_block(l2, rr, 4, own, 4)
    nine = jnp.concatenate([f, kx, ky, surf_kz], axis=0)
    total = jnp.zeros((PLANES, LANES), jnp.float32)
    for r in range(4):
        for c in range(2):
            src = lax.broadcasted_iota(jnp.int32, (LANES, LANES), 0) + c * LANES
            dst = lax.broadcasted_iota(jnp.int32, (LANES, LANES), 1) - r * 32
            pick = jnp.where((src == dst * 8) & (dst >= 0) & (dst < 32), 1.0, 0.0)
            total = total + jnp.dot(
                nine[:, c, r, :],
                pick,
                precision=lax.Precision.HIGHEST,
                preferred_element_type=jnp.float32,
            )
    pack_ref[...] = total


def whole_sweep(level, u, weights, step):
    f, kx, kx_lo, ky, kz, surf = level
    rows = u.shape[2]
    r = residual_of(
        f, u, pltpu.roll(u, rows - 1, 2), pltpu.roll(u, 1, 2), kx, kx_lo, ky, kz, surf, step
    )
    return u + weights * r, r


def up_kernel(nx, ny, x_ref, l0, l1, l2, p_ref, r_ref, g3, g4, ub, uc):
    me_x = lax.axis_index("gx")
    me_y = lax.axis_index("gy")
    tiles = ny // 4
    rows3 = nx * 4

    lane = lane_iota((rows3, LANES))
    row = lax.broadcasted_iota(jnp.int32, (rows3, LANES), 0)
    for p in range(PLANES):
        for q in range(tiles):
            if tiles == 1:
                x = x_ref[pl.ds(p, rows3, stride=PLANES), :]
            else:
                x = jnp.concatenate(
                    [
                        x_ref[pl.ds((i * ny + 4 * q) * PLANES + p, 4, stride=PLANES), :]
                        for i in range(nx)
                    ],
                    axis=0,
                )
            out = x
            for delta in range(-3, 4):
                if delta == 0:
                    continue
                moved = pltpu.roll(x, (-delta) % rows3, 0)
                moved = pltpu.roll(moved, (32 * delta) % LANES, 1)
                out = jnp.where(lane // 32 - row % 4 == delta, moved, out)
            g3[p, q, :, :] = out

    def gathered(ref):
        kx = ref[KX : KX + 2]
        return (
            ref[F : F + 2],
            kx,
            pltpu.roll(kx, 1, 2),
            ref[KY : KY + 2],
            ref[KZ : KZ + 1],
            ref[S : S + 2],
        )

    level3 = gathered(g3)
    w3 = weight(*level3[1:], 1)
    u3 = w3 * level3[0]
    u3, unused = whole_sweep(level3, u3, w3, 1)
    unused, r3 = whole_sweep(level3, u3, w3, 1)
    g4[0:2] = r3
    f, kx, ky, surf_kz = coarse_block(g3, g4, 1, 0, rows3 // 2)
    level4 = (f, kx, pltpu.roll(kx, 1, 2), ky, surf_kz[2:3], surf_kz[0:2])
    w4 = weight(*level4[1:], 2)
    u4 = w4 * f
    for step in range(CSWEEPS - 1):
        u4, unused = whole_sweep(level4, u4, w4, 2)
    unused, rc = whole_sweep(level4, u4, w4, 2)
    even = lane_iota(u4.shape) % 2 == 0

    def total(x):
        x = jnp.sum(jnp.where(even, x, 0.0), axis=(0, 1))
        return jnp.sum(jnp.sum(x, axis=0, keepdims=True), axis=1, keepdims=True)

    e4 = u4 + (total(rc) / total(level4[5]))[None, None]
    e4 = jnp.where(even, e4, from_left(e4, 1))
    put_strided(g4, 0, 0, e4)
    put_strided(g4, 0, 1, e4)
    u3 = u3 + g4[0:2]
    for step in range(POST):
        u3, unused = whole_sweep(level3, u3, w3, 1)

    rows2 = l2.shape[2] - 2 * PAD
    to_row = lax.broadcasted_iota(jnp.int32, (rows2, rows3), 0) // 2 - 4 + me_x * 4
    pick_row = jnp.where(
        to_row == lax.broadcasted_iota(jnp.int32, (rows2, rows3), 1), 1.0, 0.0
    )
    dot = functools.partial(
        jnp.dot, precision=lax.Precision.HIGHEST, preferred_element_type=jnp.float32
    )
    near = [[dot(pick_row, u3[k, q]) for q in range(tiles)] for k in range(2)]
    near = [jnp.concatenate([near[k][q] for k in range(2)], axis=0) for q in range(tiles)]
    for c in range(3):
        spread = jnp.zeros((2 * rows2, LANES), jnp.float32)
        for q in range(tiles):
            column = lax.broadcasted_iota(jnp.int32, (LANES, LANES), 1) + c * LANES
            column = jnp.where(column >= 320, column - 384, column)
            coarse = (column + 64) // 8 - 8 + me_y * 32 - q * LANES
            pick = jnp.where(
                coarse == lax.broadcasted_iota(jnp.int32, (LANES, LANES), 0), 1.0, 0.0
            )
            spread = spread + dot(near[q], pick)
        for k in range(2):
            uc[k, c, PAD : PAD + rows2, :] = spread[k * rows2 : (k + 1) * rows2]

    levels = (l0, l1, l2)
    zeros = jnp.zeros((2, 3, PAD, LANES), jnp.float32)
    for depth in (2, 1, 0):
        level = levels[depth]
        step = 1 << depth
        count = level.shape[2] - 2 * PAD
        margin = (24, 8, 0)[depth]
        starts = range(PAD + margin, PAD + count - margin, 8)
        for r0 in starts:
            put(uc, 0, r0, rows_of(uc, 0, 2, r0) + rows_of(level, U, 2, r0))
        for buf in (uc, ub):
            put(buf, 0, PAD + margin - 8, zeros)
            put(buf, 0, PAD + count - margin, zeros)
        for source, target in ((uc, ub), (ub, uc)):
            for r0 in starts:
                u, r = block_residual(level, source, 0, step, r0)
                put(target, 0, r0, u + rows_of(level, W, 2, r0) * r)
        if depth:
            finer = levels[depth - 1]
            need = (24, 8, 0)[depth - 1]
            half = step // 2
            first, last = need // 2, (finer.shape[2] - 2 * PAD - need) // 2
            blocks = []
            for r0 in range(first, last, 4):
                e = rows_of(uc, 0, 2, PAD + r0, 4)
                blocks.append(
                    jnp.where(lane_iota(e.shape) % step < half, e, from_left(e, half))
                )
            for r0, e in zip(range(first, last, 4), blocks):
                put_strided(ub, 0, PAD + 2 * r0, e)
                put_strided(ub, 0, PAD + 2 * r0 + 1, e)
            for r0 in range(PAD + need, PAD + 2 * last, 8):
                put(uc, 0, r0, rows_of(ub, 0, 2, r0))
        else:
            own = p_ref.shape[1]
            for r0 in range(0, own, 8):
                at = PAD + count // 2 - own // 2 + r0
                u, r = block_residual(level, uc, 0, step, at)
                for c in range(2):
                    p_ref[:, r0 : r0 + 8, c * LANES : (c + 1) * LANES] = u[:, c]
                    r_ref[:, r0 : r0 + 8, c * LANES : (c + 1) * LANES] = r[:, c]


def shape_of(*shape):
    return jax.ShapeDtypeStruct(shape, jnp.float32)


def vmem(*shape):
    return pltpu.VMEM(shape, jnp.float32)


def on_device(source, coef_x, coef_y, coef_z, surface):
    rows, cols = source.shape[1], source.shape[2]
    nx, ny = lax.axis_size("gx"), lax.axis_size("gy")
    row = lax.broadcasted_iota(jnp.int32, (1, rows, 1), 1)
    col = lax.broadcasted_iota(jnp.int32, (1, 1, cols), 2)
    last_row = jnp.where(lax.axis_index("gx") == nx - 1, rows - 1, -1)
    last_col = jnp.where(lax.axis_index("gy") == ny - 1, cols - 1, -1)
    kx = jnp.where(row == last_row, 0.0, coef_x)
    ky = jnp.where(col == last_col, 0.0, coef_y)
    packed = jnp.concatenate([source, kx, ky, surface, coef_z[None]], axis=0)

    near = pair_permute(packed, "gx", 0)
    far = pair_permute(packed, "gx", 1)
    params = pltpu.CompilerParams(vmem_limit_bytes=48 * 1024 * 1024)
    strips = pl.pallas_call(
        strip_kernel,
        out_shape=(shape_of(3 * rows, 2 * LANES),) * 2,
        compiler_params=params,
        name="strips",
    )(packed, near, far)
    strip_c = pair_permute(strips[0], "gy", 0)
    strip_d = pair_permute(strips[1], "gy", 1)

    heights = [3 * rows // (1 << depth) + 2 * PAD for depth in range(3)]
    planes = U + 2
    l0, l1, l2, pack = pl.pallas_call(
        down_kernel,
        out_shape=tuple(shape_of(planes, 3, h, LANES) for h in heights)
        + (shape_of(PLANES, LANES),),
        scratch_shapes=[vmem(2, 3, heights[0], LANES)] * 2,
        compiler_params=params,
        name="down",
    )(packed, near, far, strip_c, strip_d)

    devices = nx * ny
    everyone = lax.all_to_all(
        jnp.broadcast_to(pack[None], (devices, PLANES, LANES)), ("gx", "gy"), 0, 0, tiled=True
    ).reshape(devices * PLANES, LANES)

    tiles = ny // 4
    pressure, residual = pl.pallas_call(
        functools.partial(up_kernel, nx, ny),
        out_shape=(shape_of(*source.shape),) * 2,
        scratch_shapes=[
            vmem(PLANES, tiles, nx * 4, LANES),
            vmem(2, tiles, nx * 4, LANES),
            vmem(2, 3, heights[0], LANES),
            vmem(2, 3, heights[0], LANES),
        ],
        compiler_params=params,
        name="up",
    )(everyone, l0, l1, l2)
    return pressure, residual


def solution(mesh):
    layered, plane = P(None, "gx", "gy"), P("gx", "gy")
    return jax.shard_map(
        on_device,
        mesh=mesh,
        in_specs=(layered, layered, layered, plane, layered),
        out_specs=(layered, layered),
        check_vma=False,
    )
```

time: 606 us -> 51.5 us (0.08)
  blocking collectives: 324 us -> 23.2 us
  starting transfers between devices: 165 us -> 7.31 us
  waiting for transfers between devices: 84 us -> 3.67 us
  local copies, waits for them, and re-layouts: 19.5 us -> 7.04 us
  Pallas kernels: 0 us -> 7.25 us
    all_gather x5 -> x0, blocking collectives: 324 us -> none  [the longest x1 66.3 us: coarse_solve(): lax.all_gather(ky_own[None], ('gx', 'gy'), axis=0, tiled=True)]
    ppermute x70 -> x4, starting transfers between devices: 165 us -> 7.31 us  [pair_permute(): return lax.ppermute(x, axis, pairs)]
    ppermute x70 -> x4, waiting for transfers between devices: 84 us -> 3.67 us  [pair_permute(): return lax.ppermute(x, axis, pairs)]
    all_to_all x0 -> x1, blocking collectives: none -> 23.2 us  [on_device(): lax.all_to_all(jnp.broadcast_to(pack[None], (devices, PLANES, LANES)), ('...]
    slice x112 -> x0, local copies, waits for them, and re-layouts: 18 us -> none  [the longest x16 2.86 us: coarsen(): kz_c = kz[0::2, 0::2] + kz[1::2, 0::2] + kz[0::2, 1::2] + kz[1::2, 1::2]]
    pallas_call x0 -> x3, Pallas kernels: none -> 7.25 us  [the longest x1 4.61 us: on_device(): pl.pallas_call(functools.partial(up_kernel, nx, ny), out_shape=(shape_of(...]
  transfers between devices with their start and end apart: 70 -> 4, of which waited for: 42 -> 2; matrix products, arithmetic and copies ran while one was open for 2% -> 0% of each run, Pallas kernels for 0% -> 0%
where the time goes in v1:
time: 51.5 us; the launch traced here: 51 us
  blocking collectives  23.2 us (45%)
  starting transfers between devices  7.31 us (14%)
  Pallas kernels  7.25 us (14%)
  local copies, waits for them, and re-layouts  7.04 us (14%)
  waiting for transfers between devices  3.67 us (7%)
  other arithmetic  1.77 us (3%)
  between operations  0.7 us (1%)
    all_to_all x1, blocking collectives, on_device(): lax.all_to_all(jnp.broadcast_to(pack[None], (devices, PLANES, LANES)), ('...  23.2 us
    ppermute x4, starting transfers between devices, pair_permute(): return lax.ppermute(x, axis, pairs)  7.31 us
    unnamed x8, local copies, waits for them, and re-layouts  4.63 us
    pallas_call x1, Pallas kernels, on_device(): pl.pallas_call(functools.partial(up_kernel, nx, ny), out_shape=(shape_of(...  4.61 us
    ppermute x4, waiting for transfers between devices, pair_permute(): return lax.ppermute(x, axis, pairs)  3.67 us
    pallas_call x1, Pallas kernels, on_device(): pl.pallas_call(down_kernel, out_shape=tuple((shape_of(planes, 3, h, LANES...  2.35 us
    unnamed x2, other arithmetic  1.76 us
    reshape x1, local copies, waits for them, and re-layouts, on_device(): everyone = lax.all_to_all(jnp.broadcast_to(pack[None], (devices, PLANES,...  1.62 us
  transfers between devices with their start and end apart: 4, of which 2 were waited for; matrix products, arithmetic and copies ran while one was open for 0% of the time, Pallas kernels for 0%

profile of v1, /device:TPU:0, one launch (start us, length us, event | category | flops | bytes accessed | tf_op | source)
XLA Modules:
  0.0 51.0 jit_solution(11919193334056100966)
XLA Ops:
  0.7 0.8 %constant_dynamic-update-slice_fusion.1 = f32[9,32,256]{2,1,0:T(8,128)S(1)} fusion(f32[2,32,256]{2,1,0:T(8,128)} %param.5), kind=kLoop, calls=%fused_computation.4 | loop fusion | bytes 131072
  1.5 0.9 %select_dynamic-update-slice_fusion.1 = f32[9,32,256]{2,1,0:T(8,128)S(1)} fusion(f32[9,32,256]{2,1,0:T(8,128)S(1)} %constant_dynamic-update-slice_fusion.1, f32[2,32,256]{2,1,0:T(8,128)} %param.6, pred[32]{0:T(512)(128)(4,1)S(1)} %iota_compare_fusion.1), kind=kLoop, calls=%fused_computation.1 | loop fusion | flops 16384 | bytes 131584
  2.4 0.8 %select_dynamic-update-slice_fusion = f32[9,32,256]{2,1,0:T(8,128)S(1)} fusion(f32[9,32,256]{2,1,0:T(8,128)S(1)} %select_dynamic-update-slice_fusion.1, f32[2,32,256]{2,1,0:T(8,128)} %param.7, pred[256]{0:T(512)(128)(4,1)S(1)} %iota_compare_fusion), kind=kLoop, calls=%fused_computation | loop fusion | flops 16384 | bytes 131584
  3.3 0.8 %constant_dynamic-update-slice_fusion = f32[9,32,256]{2,1,0:T(8,128)S(1)} fusion(f32[9,32,256]{2,1,0:T(8,128)S(1)} %select_dynamic-update-slice_fusion, f32[2,32,256]{2,1,0:T(8,128)} %param.9), kind=kLoop, calls=%fused_computation.3 | loop fusion | bytes 131072
  4.1 0.8 %bitcast_dynamic-update-slice_fusion.own_ref = f32[9,32,256]{2,1,0:T(8,128)S(1)} fusion(f32[9,32,256]{2,1,0:T(8,128)S(1)} %constant_dynamic-update-slice_fusion, f32[32,256]{1,0:T(8,128)} %param.8), kind=kLoop, calls=%fused_computation.2 | loop fusion | bytes 65536 | tf_op jit(solution)/shard_map/concatenate | solution.py:422
  4.9 0.7 %collective-permute-start.1 = (f32[9,32,256]{2,1,0:T(8,128)S(1)}, f32[9,32,256]{2,1,0:T(8,128)S(1)}, u32[]{:S(2)}, u32[]{:S(2)}) collective-permute-start(f32[9,32,256]{2,1,0:T(8,128)S(1)} %bitcast_dynamic-update-slice_fusion.own_ref), channel_id=1, source_target_pairs={{4,8},{8,4},{12,16},{16,12},{20,24},{24,20},{5,9},{9,5},{13,17},{1... | collective-permute-start | bytes 884744 | tf_op jit(solution)/shard_map/ppermute | solution.py:29
  5.6 4.4 %collective-permute-start = (f32[9,32,256]{2,1,0:T(8,128)S(1)}, f32[9,32,256]{2,1,0:T(8,128)S(1)}, u32[]{:S(2)}, u32[]{:S(2)}) collective-permute-start(f32[9,32,256]{2,1,0:T(8,128)S(1)} %bitcast_dynamic-update-slice_fusion.own_ref), channel_id=1, source_target_pairs={{0,4},{4,0},{8,12},{12,8},{16,20},{20,16},{24,28},{28,24},{1,5},{5... | collective-permute-start | bytes 884744 | tf_op jit(solution)/shard_map/ppermute | solution.py:29
  10.0 0.0 collective-permute-done.1.far_ref
  10.0 1.2 %collective-permute-done.near_ref = f32[9,32,256]{2,1,0:T(8,128)S(1)} collective-permute-done((f32[9,32,256]{2,1,0:T(8,128)S(1)}, f32[9,32,256]{2,1,0:T(8,128)S(1)}, u32[]{:S(2)}, u32[]{:S(2)}) %collective-permute-start) | collective-permute-done | bytes 294944 | tf_op jit(solution)/shard_map/ppermute | solution.py:29
  11.2 0.3 strips.1
  11.5 1.6 %collective-permute-start.2 = (f32[96,256]{1,0:T(8,128)S(1)}, f32[96,256]{1,0:T(8,128)S(1)}, u32[]{:S(2)}, u32[]{:S(2)}) collective-permute-start(f32[96,256]{1,0:T(8,128)S(1)} %get-tuple-element.8), channel_id=1, source_target_pairs={{0,1},{1,0},{2,3},{3,2},{4,5},{5,4},{6,7},{7,6},{8,9},{9,8},{10,11... | collective-permute-start | bytes 294920 | tf_op jit(solution)/shard_map/ppermute | solution.py:29
  13.1 0.7 %collective-permute-start.3 = (f32[96,256]{1,0:T(8,128)S(1)}, f32[96,256]{1,0:T(8,128)S(1)}, u32[]{:S(2)}, u32[]{:S(2)}) collective-permute-start(f32[96,256]{1,0:T(8,128)S(1)} %get-tuple-element.9), channel_id=1, source_target_pairs={{1,2},{2,1},{5,6},{6,5},{9,10},{10,9},{13,14},{14,13},{17,18},{18,... | collective-permute-start | bytes 294920 | tf_op jit(solution)/shard_map/ppermute | solution.py:29
  13.7 2.5 %collective-permute-done.2.c_ref = f32[96,256]{1,0:T(8,128)S(1)} collective-permute-done((f32[96,256]{1,0:T(8,128)S(1)}, f32[96,256]{1,0:T(8,128)S(1)}, u32[]{:S(2)}, u32[]{:S(2)}) %collective-permute-start.2) | collective-permute-done | bytes 98336 | tf_op jit(solution)/shard_map/ppermute | solution.py:29
  16.2 0.0 collective-permute-done.3.d_ref
  16.2 2.3 %down.1 = (f32[13,3,112,128]{3,2,1,0:T(8,128)S(1)}, f32[13,3,64,128]{3,2,1,0:T(8,128)S(1)}, f32[13,3,40,128]{3,2,1,0:T(8,128)S(1)}, f32[9,128]{1,0:T(8,128)S(1)}) custom-call(f32[9,32,256]{2,1,0:T(8,128)S(1)} %bitcast_dynamic-update-slice_fusion.own_ref, f32[9,32,256]{2,1,0:T(8,128)S(1)} %collective-permute-done.near_ref, ...), custom_call_target="tpu_custom_call" | custom-call | tf_op jit(solution)/shard_map/down/pallas_call | solution.py:438
  18.5 0.0 copy-start
  18.5 0.9 %copy-done = f32[13,3,40,128]{3,2,1,0:T(8,128)} copy-done((f32[13,3,40,128]{3,2,1,0:T(8,128)}, f32[13,3,40,128]{3,2,1,0:T(8,128)S(1)}, u32[]{:S(2)}) %copy-start) | copy-done | bytes 798744
  19.5 23.2 %all_to_all.5 = f32[32,9,128]{2,1,0:T(8,128)} all-to-all(f32[32,9,128]{2,1,0:T(8,128)S(1)} %broadcast_in_dim.35), channel_id=1, replica_groups=mesh['gx'=8,'gy'=4] {'gx','gy'}, dimensions={0} | all-to-all | bytes 294912 | tf_op jit(solution)/shard_map/all_to_all | solution.py:448
  42.7 1.6 %reshape.18.x_ref = f32[288,128]{1,0:T(8,128)} reshape(f32[32,9,128]{2,1,0:T(8,128)} %all_to_all.5) | data formatting | bytes 294912 | tf_op jit(solution)/shard_map/reshape | solution.py:450
  44.3 0.0 copy-start.1
  44.3 1.1 %copy-done.1 = f32[13,3,40,128]{3,2,1,0:T(8,128)S(1)} copy-done((f32[13,3,40,128]{3,2,1,0:T(8,128)S(1)}, f32[13,3,40,128]{3,2,1,0:T(8,128)}, u32[]{:S(2)}) %copy-start.1) | copy-done | bytes 798744
  45.4 0.0 copy-start.2
  45.4 0.9 %copy-done.2 = f32[288,128]{1,0:T(8,128)S(1)} copy-done((f32[288,128]{1,0:T(8,128)S(1)}, f32[288,128]{1,0:T(8,128)}, u32[]{:S(2)}) %copy-start.2) | copy-done | bytes 147480
  46.3 4.6 %up.1 = (f32[2,32,256]{2,1,0:T(8,128)}, f32[2,32,256]{2,1,0:T(8,128)}) custom-call(f32[288,128]{1,0:T(8,128)S(1)} %copy-done.2, f32[13,3,112,128]{3,2,1,0:T(8,128)S(1)} %get-tuple-element.11.l0, f32[13,3,64,128]{3,2,1,0:T(8,128)S(1)} %get-tuple-element.12.l1, f32[13,3,40,128]{3,2,1,0:T(8,128)S(1)} %copy-done.1), custom_call_target="tpu_custom_call" | custom-call | tf_op jit(solution)/shard_map/up/pallas_call | solution.py:453
  (3 shorter events, 0.0 us)
Async XLA Ops:
  4.9 5.1 %collective-permute-start.1 = (f32[9,32,256]{2,1,0:T(8,128)S(1)}, f32[9,32,256]{2,1,0:T(8,128)S(1)}, u32[]{:S(2)}, u32[]{:S(2)}) collective-permute-start(f32[9,32,256]{2,1,0:T(8,128)S(1)} %bitcast_dynamic-update-slice_fusion.own_ref), channel_id=1, source_target_pairs={{4,8},{8,4},{12,16},{16,12},{20,24},{24,20},{5,9},{9,5},{13,17},{1... | collective-permute-start | bytes 884744 | tf_op jit(solution)/shard_map/ppermute | solution.py:29
  5.6 5.6 %collective-permute-start = (f32[9,32,256]{2,1,0:T(8,128)S(1)}, f32[9,32,256]{2,1,0:T(8,128)S(1)}, u32[]{:S(2)}, u32[]{:S(2)}) collective-permute-start(f32[9,32,256]{2,1,0:T(8,128)S(1)} %bitcast_dynamic-update-slice_fusion.own_ref), channel_id=1, source_target_pairs={{0,4},{4,0},{8,12},{12,8},{16,20},{20,16},{24,28},{28,24},{1,5},{5... | collective-permute-start | bytes 884744 | tf_op jit(solution)/shard_map/ppermute | solution.py:29
  11.5 4.7 %collective-permute-start.2 = (f32[96,256]{1,0:T(8,128)S(1)}, f32[96,256]{1,0:T(8,128)S(1)}, u32[]{:S(2)}, u32[]{:S(2)}) collective-permute-start(f32[96,256]{1,0:T(8,128)S(1)} %get-tuple-element.8), channel_id=1, source_target_pairs={{0,1},{1,0},{2,3},{3,2},{4,5},{5,4},{6,7},{7,6},{8,9},{9,8},{10,11... | collective-permute-start | bytes 294920 | tf_op jit(solution)/shard_map/ppermute | solution.py:29
  13.1 3.1 %collective-permute-start.3 = (f32[96,256]{1,0:T(8,128)S(1)}, f32[96,256]{1,0:T(8,128)S(1)}, u32[]{:S(2)}, u32[]{:S(2)}) collective-permute-start(f32[96,256]{1,0:T(8,128)S(1)} %get-tuple-element.9), channel_id=1, source_target_pairs={{1,2},{2,1},{5,6},{6,5},{9,10},{10,9},{13,14},{14,13},{17,18},{18,... | collective-permute-start | bytes 294920 | tf_op jit(solution)/shard_map/ppermute | solution.py:29
  18.5 0.9 %copy-start = (f32[13,3,40,128]{3,2,1,0:T(8,128)}, f32[13,3,40,128]{3,2,1,0:T(8,128)S(1)}, u32[]{:S(2)}) copy-start(f32[13,3,40,128]{3,2,1,0:T(8,128)S(1)} %get-tuple-element.13.l2) | copy-start | bytes 2396164
  44.3 1.1 %copy-start.1 = (f32[13,3,40,128]{3,2,1,0:T(8,128)S(1)}, f32[13,3,40,128]{3,2,1,0:T(8,128)}, u32[]{:S(2)}) copy-start(f32[13,3,40,128]{3,2,1,0:T(8,128)} %copy-done) | copy-start | bytes 2396164
  45.4 0.9 %copy-start.2 = (f32[288,128]{1,0:T(8,128)S(1)}, f32[288,128]{1,0:T(8,128)}, u32[]{:S(2)}) copy-start(f32[288,128]{1,0:T(8,128)} %reshape.18.x_ref) | copy-start | bytes 442372

commit v2 on v1

--- a/solution.py
+++ b/solution.py
@@ -17,6 +17,7 @@
 WIDTH = 28
 PAD = 8
 PLANES = 9
+PACK = 16
 F, KX, KY, S, KZ = 0, 2, 4, 6, 8
 W, U = 9, 11
 
@@ -129,6 +130,28 @@
     low = jnp.where(is_even, other, mine)
     high = jnp.where(is_even, mine, other)
     return low, high
+
+
+def pack_kernel(source, coef_x, coef_y, surface, coef_z, out, sems):
+    inputs = ((source, F, 2), (coef_x, KX, 2), (coef_y, KY, 2), (surface, S, 2), (coef_z, KZ, 0))
+    copies = []
+    for k, (ref, plane, count) in enumerate(inputs):
+        to = out.at[plane : plane + count] if count else out.at[plane]
+        copies.append(pltpu.make_async_copy(ref, to, sems.at[k]))
+    for copy in copies:
+        copy.start()
+    for copy in copies:
+        copy.wait()
+    rows, cols = out.shape[1], out.shape[2]
+    wall_x = lax.axis_index("gx") == lax.axis_size("gx") - 1
+    wall_y = lax.axis_index("gy") == lax.axis_size("gy") - 1
+    edge = out[KX : KX + 2, rows - 8 :, :]
+    row = lax.broadcasted_iota(jnp.int32, edge.shape, 1)
+    out[KX : KX + 2, rows - 8 :, :] = jnp.where(wall_x & (row == 7), 0.0, edge)
+    edge = out[KY : KY + 2, :, cols - LANES :]
+    out[KY : KY + 2, :, cols - LANES :] = jnp.where(
+        wall_y & (lane_iota(edge.shape) == LANES - 1), 0.0, edge
+    )
 
 
 def strip_kernel(own_ref, near_ref, far_ref, c_ref, d_ref):
@@ -257,7 +280,8 @@
                 precision=lax.Precision.HIGHEST,
                 preferred_element_type=jnp.float32,
             )
-    pack_ref[...] = total
+    pack_ref[0, 0:PLANES, :] = total
+    pack_ref[0, PLANES:PACK, :] = jnp.zeros((PACK - PLANES, LANES), jnp.float32)
 
 
 def whole_sweep(level, u, weights, step):
@@ -269,22 +293,26 @@
     return u + weights * r, r
 
 
-def up_kernel(nx, ny, x_ref, l0, l1, l2, p_ref, r_ref, g3, g4, ub, uc):
+def up_kernel(nx, ny, x_ref, l0, l1, l2, p_ref, r_ref, xs, g3, g4, ub, uc, sem):
     me_x = lax.axis_index("gx")
     me_y = lax.axis_index("gy")
     tiles = ny // 4
     rows3 = nx * 4
+
+    copy = pltpu.make_async_copy(x_ref, xs, sem)
+    copy.start()
+    copy.wait()
 
     lane = lane_iota((rows3, LANES))
     row = lax.broadcasted_iota(jnp.int32, (rows3, LANES), 0)
     for p in range(PLANES):
         for q in range(tiles):
             if tiles == 1:
-                x = x_ref[pl.ds(p, rows3, stride=PLANES), :]
+                x = xs[pl.ds(p, rows3, stride=PACK), :]
             else:
                 x = jnp.concatenate(
                     [
-                        x_ref[pl.ds((i * ny + 4 * q) * PLANES + p, 4, stride=PLANES), :]
+                        xs[pl.ds((i * ny + 4 * q) * PACK + p, 4, stride=PACK), :]
                         for i in range(nx)
                     ],
                     axis=0,
@@ -413,17 +441,23 @@
 def on_device(source, coef_x, coef_y, coef_z, surface):
     rows, cols = source.shape[1], source.shape[2]
     nx, ny = lax.axis_size("gx"), lax.axis_size("gy")
-    row = lax.broadcasted_iota(jnp.int32, (1, rows, 1), 1)
-    col = lax.broadcasted_iota(jnp.int32, (1, 1, cols), 2)
-    last_row = jnp.where(lax.axis_index("gx") == nx - 1, rows - 1, -1)
-    last_col = jnp.where(lax.axis_index("gy") == ny - 1, cols - 1, -1)
-    kx = jnp.where(row == last_row, 0.0, coef_x)
-    ky = jnp.where(col == last_col, 0.0, coef_y)
-    packed = jnp.concatenate([source, kx, ky, surface, coef_z[None]], axis=0)
+    params = pltpu.CompilerParams(vmem_limit_bytes=24 * 1024 * 1024)
+    packed = pl.pallas_call(
+        pack_kernel,
+        out_shape=shape_of(PLANES, rows, cols),
+        in_specs=[pl.BlockSpec(memory_space=pltpu.HBM)] * 5,
+        scratch_shapes=[pltpu.SemaphoreType.DMA((5,))],
+        compiler_params=params,
+        name="pack",
+    )(
+        *(
+            pltpu.with_memory_space_constraint(x, pltpu.HBM)
+            for x in (source, coef_x, coef_y, surface, coef_z)
+        )
+    )
 
     near = pair_permute(packed, "gx", 0)
     far = pair_permute(packed, "gx", 1)
-    params = pltpu.CompilerParams(vmem_limit_bytes=48 * 1024 * 1024)
     strips = pl.pallas_call(
         strip_kernel,
         out_shape=(shape_of(3 * rows, 2 * LANES),) * 2,
@@ -438,30 +472,33 @@
     l0, l1, l2, pack = pl.pallas_call(
         down_kernel,
         out_shape=tuple(shape_of(planes, 3, h, LANES) for h in heights)
-        + (shape_of(PLANES, LANES),),
+        + (shape_of(1, PACK, LANES),),
         scratch_shapes=[vmem(2, 3, heights[0], LANES)] * 2,
         compiler_params=params,
         name="down",
     )(packed, near, far, strip_c, strip_d)
 
-    devices = nx * ny
     everyone = lax.all_to_all(
-        jnp.broadcast_to(pack[None], (devices, PLANES, LANES)), ("gx", "gy"), 0, 0, tiled=True
-    ).reshape(devices * PLANES, LANES)
+        jnp.broadcast_to(pack, (nx * ny, PACK, LANES)), ("gx", "gy"), 0, 0, tiled=True
+    ).reshape(nx * ny * PACK, LANES)
 
     tiles = ny // 4
     pressure, residual = pl.pallas_call(
         functools.partial(up_kernel, nx, ny),
         out_shape=(shape_of(*source.shape),) * 2,
         scratch_shapes=[
+            vmem(nx * ny * PACK, LANES),
             vmem(PLANES, tiles, nx * 4, LANES),
             vmem(2, tiles, nx * 4, LANES),
             vmem(2, 3, heights[0], LANES),
             vmem(2, 3, heights[0], LANES),
+            pltpu.SemaphoreType.DMA,
         ],
+        in_specs=[pl.BlockSpec(memory_space=pltpu.HBM)]
+        + [pl.BlockSpec(memory_space=pltpu.VMEM)] * 3,
         compiler_params=params,
         name="up",
-    )(everyone, l0, l1, l2)
+    )(pltpu.with_memory_space_constraint(everyone, pltpu.HBM), l0, l1, l2)
     return pressure, residual
 
 

time: 51.5 us -> 44.5 us (0.86)
  local copies, waits for them, and re-layouts: 7.04 us -> 0.03 us
  Pallas kernels: 7.25 us -> 9.35 us
  other arithmetic: 1.77 us -> 0 us
    unnamed x8 -> x0, local copies, waits for them, and re-layouts: 4.63 us -> none
    unnamed x2 -> x0, other arithmetic: 1.76 us -> none
    reshape x1 -> x0, local copies, waits for them, and re-layouts: 1.62 us -> none  [on_device(): everyone = lax.all_to_all(jnp.broadcast_to(pack[None], (devices, PLANES,...]
    pallas_call x1, Pallas kernels: 4.61 us -> 5.63 us  [on_device(): pl.pallas_call(functools.partial(up_kernel, nx, ny), out_shape=(shape_of(...]
    pallas_call x0 -> x1, Pallas kernels: none -> 0.99 us  [on_device(): pl.pallas_call(pack_kernel, out_shape=shape_of(PLANES, rows, cols), in_sp...]
    concatenate x1 -> x0, local copies, waits for them, and re-layouts: 0.76 us -> none  [on_device(): packed = jnp.concatenate([source, kx, ky, surface, coef_z[None]], axis=0)]
where the time goes in v2:
time: 44.5 us; the launch traced here: 44.3 us
  blocking collectives  23.2 us (52%)
  Pallas kernels  9.35 us (21%)
  starting transfers between devices  7.32 us (16%)
  waiting for transfers between devices  3.67 us (8%)
  between operations  0.67 us (2%)
    all_to_all x1, blocking collectives, on_device(): lax.all_to_all(jnp.broadcast_to(pack, (nx * ny, PACK, LANES)), ('gx', 'gy...  23.2 us
    ppermute x4, starting transfers between devices, pair_permute(): return lax.ppermute(x, axis, pairs)  7.32 us
    pallas_call x1, Pallas kernels, on_device(): pl.pallas_call(functools.partial(up_kernel, nx, ny), out_shape=(shape_of(...  5.63 us
    ppermute x4, waiting for transfers between devices, pair_permute(): return lax.ppermute(x, axis, pairs)  3.67 us
    pallas_call x1, Pallas kernels, on_device(): pl.pallas_call(down_kernel, out_shape=tuple((shape_of(planes, 3, h, LANES...  2.44 us
    pallas_call x1, Pallas kernels, on_device(): pl.pallas_call(pack_kernel, out_shape=shape_of(PLANES, rows, cols), in_sp...  0.99 us
  transfers between devices with their start and end apart: 4, of which 2 were waited for; matrix products, arithmetic and copies ran while one was open for 0% of the time, Pallas kernels for 0%

profile of v2, /device:TPU:0, one launch (start us, length us, event | category | flops | bytes accessed | tf_op | source)
XLA Modules:
  0.0 44.3 jit_solution(3432739796485400380)
XLA Ops:
  0.6 1.0 %pack.1.own_ref = f32[9,32,256]{2,1,0:T(8,128)S(1)} custom-call(f32[2,32,256]{2,1,0:T(8,128)} %source.1, f32[2,32,256]{2,1,0:T(8,128)} %coef_x.1, f32[2,32,256]{2,1,0:T(8,128)} %coef_y.1, f32[2,32,256]{2,1,0:T(8,128)} %surface.1, f32[32,256]{1,0:T(8,128)} %coef_z.1), custom_call_target="tpu_custom_call" | custom-call | tf_op jit(solution)/shard_map/pack/pallas_call | solution.py:445
  1.6 0.7 %collective-permute-start.1 = (f32[9,32,256]{2,1,0:T(8,128)S(1)}, f32[9,32,256]{2,1,0:T(8,128)S(1)}, u32[]{:S(2)}, u32[]{:S(2)}) collective-permute-start(f32[9,32,256]{2,1,0:T(8,128)S(1)} %pack.1.own_ref), channel_id=1, source_target_pairs={{4,8},{8,4},{12,16},{16,12},{20,24},{24,20},{5,9},{9,5},{13,17},{1... | collective-permute-start | bytes 884744 | tf_op jit(solution)/shard_map/ppermute | solution.py:30
  2.3 4.4 %collective-permute-start = (f32[9,32,256]{2,1,0:T(8,128)S(1)}, f32[9,32,256]{2,1,0:T(8,128)S(1)}, u32[]{:S(2)}, u32[]{:S(2)}) collective-permute-start(f32[9,32,256]{2,1,0:T(8,128)S(1)} %pack.1.own_ref), channel_id=1, source_target_pairs={{0,4},{4,0},{8,12},{12,8},{16,20},{20,16},{24,28},{28,24},{1,5},{5... | collective-permute-start | bytes 884744 | tf_op jit(solution)/shard_map/ppermute | solution.py:30
  6.7 0.0 collective-permute-done.1.far_ref
  6.8 1.2 %collective-permute-done.near_ref = f32[9,32,256]{2,1,0:T(8,128)S(1)} collective-permute-done((f32[9,32,256]{2,1,0:T(8,128)S(1)}, f32[9,32,256]{2,1,0:T(8,128)S(1)}, u32[]{:S(2)}, u32[]{:S(2)}) %collective-permute-start) | collective-permute-done | bytes 294944 | tf_op jit(solution)/shard_map/ppermute | solution.py:30
  8.0 0.3 strips.1
  8.3 1.6 %collective-permute-start.2 = (f32[96,256]{1,0:T(8,128)S(1)}, f32[96,256]{1,0:T(8,128)S(1)}, u32[]{:S(2)}, u32[]{:S(2)}) collective-permute-start(f32[96,256]{1,0:T(8,128)S(1)} %get-tuple-element.8), channel_id=1, source_target_pairs={{0,1},{1,0},{2,3},{3,2},{4,5},{5,4},{6,7},{7,6},{8,9},{9,8},{10,11... | collective-permute-start | bytes 294920 | tf_op jit(solution)/shard_map/ppermute | solution.py:30
  9.8 0.7 %collective-permute-start.3 = (f32[96,256]{1,0:T(8,128)S(1)}, f32[96,256]{1,0:T(8,128)S(1)}, u32[]{:S(2)}, u32[]{:S(2)}) collective-permute-start(f32[96,256]{1,0:T(8,128)S(1)} %get-tuple-element.9), channel_id=1, source_target_pairs={{1,2},{2,1},{5,6},{6,5},{9,10},{10,9},{13,14},{14,13},{17,18},{18,... | collective-permute-start | bytes 294920 | tf_op jit(solution)/shard_map/ppermute | solution.py:30
  10.5 2.5 %collective-permute-done.2.c_ref = f32[96,256]{1,0:T(8,128)S(1)} collective-permute-done((f32[96,256]{1,0:T(8,128)S(1)}, f32[96,256]{1,0:T(8,128)S(1)}, u32[]{:S(2)}, u32[]{:S(2)}) %collective-permute-start.2) | collective-permute-done | bytes 98336 | tf_op jit(solution)/shard_map/ppermute | solution.py:30
  12.9 0.0 collective-permute-done.3.d_ref
  12.9 2.4 %down.1 = (f32[13,3,112,128]{3,2,1,0:T(8,128)S(1)}, f32[13,3,64,128]{3,2,1,0:T(8,128)S(1)}, f32[13,3,40,128]{3,2,1,0:T(8,128)S(1)}, f32[1,16,128]{2,1,0:T(8,128)S(1)}) custom-call(f32[9,32,256]{2,1,0:T(8,128)S(1)} %pack.1.own_ref, f32[9,32,256]{2,1,0:T(8,128)S(1)} %collective-permute-done.near_ref, f32[9,32,256]{2,1,0:T(8,128)S(1)} %collective-permute-done.1.far_ref, ...), custom_call_target="tpu_custom_call" | custom-call | tf_op jit(solution)/shard_map/down/pallas_call | solution.py:472
  15.4 23.2 %all_to_all.5 = f32[32,16,128]{2,1,0:T(8,128)} all-to-all(f32[32,16,128]{2,1,0:T(8,128)S(1)} %broadcast_in_dim.8), channel_id=1, replica_groups=mesh['gx'=8,'gy'=4] {'gx','gy'}, dimensions={0} | all-to-all | bytes 524288 | tf_op jit(solution)/shard_map/all_to_all | solution.py:481
  38.6 5.6 %up.1 = (f32[2,32,256]{2,1,0:T(8,128)}, f32[2,32,256]{2,1,0:T(8,128)}) custom-call(f32[512,128]{1,0:T(8,128)} %bitcast.3, f32[13,3,112,128]{3,2,1,0:T(8,128)S(1)} %get-tuple-element.11.l0, f32[13,3,64,128]{3,2,1,0:T(8,128)S(1)} %get-tuple-element.12.l1, f32[13,3,40,128]{3,2,1,0:T(8,128)S(1)} %get-tuple-element.13.l2), custom_call_target="tpu_custom_call" | custom-call | tf_op jit(solution)/shard_map/up/pallas_call | solution.py:486
  (1 shorter events, 0.0 us)
Async XLA Ops:
  1.6 5.1 %collective-permute-start.1 = (f32[9,32,256]{2,1,0:T(8,128)S(1)}, f32[9,32,256]{2,1,0:T(8,128)S(1)}, u32[]{:S(2)}, u32[]{:S(2)}) collective-permute-start(f32[9,32,256]{2,1,0:T(8,128)S(1)} %pack.1.own_ref), channel_id=1, source_target_pairs={{4,8},{8,4},{12,16},{16,12},{20,24},{24,20},{5,9},{9,5},{13,17},{1... | collective-permute-start | bytes 884744 | tf_op jit(solution)/shard_map/ppermute | solution.py:30
  2.3 5.6 %collective-permute-start = (f32[9,32,256]{2,1,0:T(8,128)S(1)}, f32[9,32,256]{2,1,0:T(8,128)S(1)}, u32[]{:S(2)}, u32[]{:S(2)}) collective-permute-start(f32[9,32,256]{2,1,0:T(8,128)S(1)} %pack.1.own_ref), channel_id=1, source_target_pairs={{0,4},{4,0},{8,12},{12,8},{16,20},{20,16},{24,28},{28,24},{1,5},{5... | collective-permute-start | bytes 884744 | tf_op jit(solution)/shard_map/ppermute | solution.py:30
  8.3 4.7 %collective-permute-start.2 = (f32[96,256]{1,0:T(8,128)S(1)}, f32[96,256]{1,0:T(8,128)S(1)}, u32[]{:S(2)}, u32[]{:S(2)}) collective-permute-start(f32[96,256]{1,0:T(8,128)S(1)} %get-tuple-element.8), channel_id=1, source_target_pairs={{0,1},{1,0},{2,3},{3,2},{4,5},{5,4},{6,7},{7,6},{8,9},{9,8},{10,11... | collective-permute-start | bytes 294920 | tf_op jit(solution)/shard_map/ppermute | solution.py:30
  9.8 3.1 %collective-permute-start.3 = (f32[96,256]{1,0:T(8,128)S(1)}, f32[96,256]{1,0:T(8,128)S(1)}, u32[]{:S(2)}, u32[]{:S(2)}) collective-permute-start(f32[96,256]{1,0:T(8,128)S(1)} %get-tuple-element.9), channel_id=1, source_target_pairs={{1,2},{2,1},{5,6},{6,5},{9,10},{10,9},{13,14},{14,13},{17,18},{18,... | collective-permute-start | bytes 294920 | tf_op jit(solution)/shard_map/ppermute | solution.py:30

commit v3 on v2

--- a/solution.py
+++ b/solution.py
@@ -17,17 +17,27 @@
 WIDTH = 28
 PAD = 8
 PLANES = 9
-PACK = 16
+PACK = PLANES * LANES
 F, KX, KY, S, KZ = 0, 2, 4, 6, 8
 W, U = 9, 11
 
 
-def pair_permute(x, axis, first):
+def pair_permute(x, axis, first, wrap=False):
     count = lax.axis_size(axis)
     pairs = []
-    for i in range(first, count - 1, 2):
-        pairs += [(i, i + 1), (i + 1, i)]
+    for i in range(first, count if wrap else count - 1, 2):
+        pairs += [(i, (i + 1) % count), ((i + 1) % count, i)]
     return lax.ppermute(x, axis, pairs)
+
+
+def far_permute(x):
+    nx, ny = lax.axis_size("gx"), lax.axis_size("gy")
+    pairs = []
+    for i in range(nx):
+        for j in range(ny):
+            to = (i, j ^ 2) if i in (0, nx - 1) else (((i - 1) ^ 1) + 1, j)
+            pairs.append((i * ny + j, to[0] * ny + to[1]))
+    return lax.ppermute(x, ("gx", "gy"), pairs)
 
 
 def lane_iota(shape):
@@ -132,7 +142,13 @@
     return low, high
 
 
-def pack_kernel(source, coef_x, coef_y, surface, coef_z, out, sems):
+def sides_x(near, far):
+    me = lax.axis_index("gx")
+    low, high = sides(near, far, lax.rem(me, 2) == 0)
+    return jnp.where(me == 0, 0.0, low), high
+
+
+def pack_kernel(source, coef_x, coef_y, surface, coef_z, out, c_ref, d_ref, sems):
     inputs = ((source, F, 2), (coef_x, KX, 2), (coef_y, KY, 2), (surface, S, 2), (coef_z, KZ, 0))
     copies = []
     for k, (ref, plane, count) in enumerate(inputs):
@@ -153,45 +169,29 @@
         wall_y & (lane_iota(edge.shape) == LANES - 1), 0.0, edge
     )
 
-
-def strip_kernel(own_ref, near_ref, far_ref, c_ref, d_ref):
-    even_x = lax.rem(lax.axis_index("gx"), 2) == 0
     even_y = lax.rem(lax.axis_index("gy"), 2) == 0
-    rows = own_ref.shape[1]
-    cols = own_ref.shape[2]
     lane = lane_iota((8, LANES))
-
-    def place(pieces, offset):
-        tiles = [jnp.zeros((8, LANES), jnp.float32)] * 2
+    for r0 in range(0, rows, 8):
+        left = [jnp.zeros((8, LANES), jnp.float32)] * 2
+        right = list(left)
         for p in range(PLANES):
             begin = p * WIDTH
-            rolled = pltpu.roll(pieces[p], (begin - offset) % LANES, 1)
-            for a in range(2):
-                lo, hi = begin - a * LANES, begin + WIDTH - a * LANES
-                if hi > 0 and lo < LANES:
-                    tiles[a] = jnp.where((lane >= lo) & (lane < hi), rolled, tiles[a])
-        return tiles
-
-    for block in range(3 * rows // 8):
-        part, r0 = divmod(block * 8, rows)
-        first, last = [], []
-        for p in range(PLANES):
-            for held, column in ((first, 0), (last, cols - LANES)):
-                at = (p, slice(r0, r0 + 8), slice(column, column + LANES))
-                if part == 1:
-                    held.append(own_ref[at])
-                else:
-                    held.append(sides(near_ref[at], far_ref[at], even_x)[part // 2])
-        left = place(first, 0)
-        right = place(last, LANES - WIDTH)
+            for tiles, column, offset in ((left, 0, 0), (right, cols - LANES, LANES - WIDTH)):
+                piece = out[p, r0 : r0 + 8, column : column + LANES]
+                rolled = pltpu.roll(piece, (begin - offset) % LANES, 1)
+                for a in range(2):
+                    lo, hi = begin - a * LANES, begin + WIDTH - a * LANES
+                    if hi > 0 and lo < LANES:
+                        tiles[a] = jnp.where((lane >= lo) & (lane < hi), rolled, tiles[a])
         for a in range(2):
-            at = (slice(block * 8, block * 8 + 8), slice(a * LANES, (a + 1) * LANES))
+            at = (slice(r0, r0 + 8), slice(a * LANES, (a + 1) * LANES))
             c_ref[at] = jnp.where(even_y, right[a], left[a])
             d_ref[at] = jnp.where(even_y, left[a], right[a])
 
 
-def down_kernel(own_ref, near_ref, far_ref, c_ref, d_ref, l0, l1, l2, pack_ref, ua, rr):
-    even_x = lax.rem(lax.axis_index("gx"), 2) == 0
+def down_kernel(
+    own_ref, near_ref, far_ref, own_cd, near_cd, far_cd, l0, l1, l2, pack_ref, ua, rr
+):
     even_y = lax.rem(lax.axis_index("gy"), 2) == 0
     rows = own_ref.shape[1]
     lane = lane_iota((8, LANES))
@@ -213,11 +213,17 @@
                 if part == 1:
                     l0[p, c, to, :] = own_ref[at]
                 else:
-                    l0[p, c, to, :] = sides(near_ref[at], far_ref[at], even_x)[part // 2]
+                    l0[p, c, to, :] = sides_x(near_ref[at], far_ref[at])[part // 2]
         low, high = [], []
         for a in range(2):
-            at = (slice(block * 8, block * 8 + 8), slice(a * LANES, (a + 1) * LANES))
-            lo, hi = sides(c_ref[at], d_ref[at], even_y)
+            held = []
+            for base in (0, rows):
+                at = (slice(base + r0, base + r0 + 8), slice(a * LANES, (a + 1) * LANES))
+                if part == 1:
+                    held.append(own_cd[at])
+                else:
+                    held.append(sides_x(near_cd[at], far_cd[at])[part // 2])
+            lo, hi = sides(held[0], held[1], even_y)
             low.append(lo)
             high.append(hi)
         for p in range(PLANES):
@@ -280,8 +286,11 @@
                 precision=lax.Precision.HIGHEST,
                 preferred_element_type=jnp.float32,
             )
-    pack_ref[0, 0:PLANES, :] = total
-    pack_ref[0, PLANES:PACK, :] = jnp.zeros((PACK - PLANES, LANES), jnp.float32)
+    for p in range(PLANES):
+        at = slice(p * LANES, (p + 1) * LANES)
+        pack_ref[:, :, at] = jnp.broadcast_to(
+            total[p : p + 1][None], (pack_ref.shape[0], 1, LANES)
+        )
 
 
 def whole_sweep(level, u, weights, step):
@@ -293,26 +302,22 @@
     return u + weights * r, r
 
 
-def up_kernel(nx, ny, x_ref, l0, l1, l2, p_ref, r_ref, xs, g3, g4, ub, uc, sem):
+def up_kernel(nx, ny, x_ref, l0, l1, l2, p_ref, r_ref, g3, g4, ub, uc):
     me_x = lax.axis_index("gx")
     me_y = lax.axis_index("gy")
     tiles = ny // 4
     rows3 = nx * 4
-
-    copy = pltpu.make_async_copy(x_ref, xs, sem)
-    copy.start()
-    copy.wait()
 
     lane = lane_iota((rows3, LANES))
     row = lax.broadcasted_iota(jnp.int32, (rows3, LANES), 0)
     for p in range(PLANES):
         for q in range(tiles):
             if tiles == 1:
-                x = xs[pl.ds(p, rows3, stride=PACK), :]
+                x = x_ref[pl.ds(p, rows3, stride=PLANES), :]
             else:
                 x = jnp.concatenate(
                     [
-                        xs[pl.ds((i * ny + 4 * q) * PACK + p, 4, stride=PACK), :]
+                        x_ref[pl.ds((i * ny + 4 * q) * PLANES + p, 4, stride=PLANES), :]
                         for i in range(nx)
                     ],
                     axis=0,
@@ -442,9 +447,9 @@
     rows, cols = source.shape[1], source.shape[2]
     nx, ny = lax.axis_size("gx"), lax.axis_size("gy")
     params = pltpu.CompilerParams(vmem_limit_bytes=24 * 1024 * 1024)
-    packed = pl.pallas_call(
+    packed, strip_c, strip_d = pl.pallas_call(
         pack_kernel,
-        out_shape=shape_of(PLANES, rows, cols),
+        out_shape=(shape_of(PLANES, rows, cols),) + (shape_of(rows, 2 * LANES),) * 2,
         in_specs=[pl.BlockSpec(memory_space=pltpu.HBM)] * 5,
         scratch_shapes=[pltpu.SemaphoreType.DMA((5,))],
         compiler_params=params,
@@ -456,49 +461,41 @@
         )
     )
 
+    strip_c = pair_permute(strip_c, "gy", 0)
+    strip_d = pair_permute(strip_d, "gy", 1, wrap=True)
+    far = far_permute(packed)
     near = pair_permute(packed, "gx", 0)
-    far = pair_permute(packed, "gx", 1)
-    strips = pl.pallas_call(
-        strip_kernel,
-        out_shape=(shape_of(3 * rows, 2 * LANES),) * 2,
-        compiler_params=params,
-        name="strips",
-    )(packed, near, far)
-    strip_c = pair_permute(strips[0], "gy", 0)
-    strip_d = pair_permute(strips[1], "gy", 1)
+    strips = jnp.concatenate([strip_c, strip_d], axis=0)
+    far_strips = far_permute(strips)
+    near_strips = pair_permute(strips, "gx", 0)
 
     heights = [3 * rows // (1 << depth) + 2 * PAD for depth in range(3)]
     planes = U + 2
     l0, l1, l2, pack = pl.pallas_call(
         down_kernel,
         out_shape=tuple(shape_of(planes, 3, h, LANES) for h in heights)
-        + (shape_of(1, PACK, LANES),),
+        + (shape_of(nx * ny, 1, PACK),),
         scratch_shapes=[vmem(2, 3, heights[0], LANES)] * 2,
         compiler_params=params,
         name="down",
-    )(packed, near, far, strip_c, strip_d)
-
-    everyone = lax.all_to_all(
-        jnp.broadcast_to(pack, (nx * ny, PACK, LANES)), ("gx", "gy"), 0, 0, tiled=True
-    ).reshape(nx * ny * PACK, LANES)
+    )(packed, near, far, strips, near_strips, far_strips)
+
+    everyone = lax.all_to_all(pack, ("gx", "gy"), 0, 0, tiled=True)
+    everyone = everyone.reshape(nx * ny * PLANES, LANES)
 
     tiles = ny // 4
     pressure, residual = pl.pallas_call(
         functools.partial(up_kernel, nx, ny),
         out_shape=(shape_of(*source.shape),) * 2,
         scratch_shapes=[
-            vmem(nx * ny * PACK, LANES),
             vmem(PLANES, tiles, nx * 4, LANES),
             vmem(2, tiles, nx * 4, LANES),
             vmem(2, 3, heights[0], LANES),
             vmem(2, 3, heights[0], LANES),
-            pltpu.SemaphoreType.DMA,
         ],
-        in_specs=[pl.BlockSpec(memory_space=pltpu.HBM)]
-        + [pl.BlockSpec(memory_space=pltpu.VMEM)] * 3,
         compiler_params=params,
         name="up",
-    )(pltpu.with_memory_space_constraint(everyone, pltpu.HBM), l0, l1, l2)
+    )(everyone, l0, l1, l2)
     return pressure, residual
 
 

time: 44.5 us -> 34.7 us (0.78)
  blocking collectives: 23.2 us -> 11.7 us
  waiting for transfers between devices: 3.67 us -> 5.98 us
  Pallas kernels: 9.35 us -> 8.33 us
  starting transfers between devices: 7.32 us -> 7.84 us
    all_to_all x1, blocking collectives: 23.2 us -> 11.7 us  [on_device(): everyone = lax.all_to_all(pack, ('gx', 'gy'), 0, 0, tiled=True)]
    ppermute x0 -> x2, starting transfers between devices: none -> 3.1 us  [far_permute(): return lax.ppermute(x, ('gx', 'gy'), pairs)]
    ppermute x0 -> x2, waiting for transfers between devices: none -> 2.62 us  [far_permute(): return lax.ppermute(x, ('gx', 'gy'), pairs)]
    ppermute x4, starting transfers between devices: 7.32 us -> 4.73 us  [pair_permute(): return lax.ppermute(x, axis, pairs)]
    pallas_call x1, Pallas kernels: 5.63 us -> 4.68 us  [on_device(): pl.pallas_call(functools.partial(up_kernel, nx, ny), out_shape=(shape_of(...]
    pallas_call x2 -> x1, Pallas kernels: 1.28 us -> 1.12 us  [on_device(): pl.pallas_call(pack_kernel, out_shape=(shape_of(PLANES, rows, cols),) + (...]
  transfers between devices with their start and end apart: 4 -> 6, of which waited for: 2 -> 2; matrix products, arithmetic and copies ran while one was open for 0% -> 0% of each run, Pallas kernels for 0% -> 0%
where the time goes in v3:
time: 34.7 us; the launch traced here: 34.5 us
  blocking collectives  11.7 us (34%)
  Pallas kernels  8.33 us (24%)
  starting transfers between devices  7.84 us (23%)
  waiting for transfers between devices  5.98 us (17%)
  between operations  0.66 us (2%)
    all_to_all x1, blocking collectives, on_device(): everyone = lax.all_to_all(pack, ('gx', 'gy'), 0, 0, tiled=True)  11.7 us
    ppermute x4, starting transfers between devices, pair_permute(): return lax.ppermute(x, axis, pairs)  4.73 us
    pallas_call x1, Pallas kernels, on_device(): pl.pallas_call(functools.partial(up_kernel, nx, ny), out_shape=(shape_of(...  4.68 us
    ppermute x4, waiting for transfers between devices, pair_permute(): return lax.ppermute(x, axis, pairs)  3.37 us
    ppermute x2, starting transfers between devices, far_permute(): return lax.ppermute(x, ('gx', 'gy'), pairs)  3.1 us
    ppermute x2, waiting for transfers between devices, far_permute(): return lax.ppermute(x, ('gx', 'gy'), pairs)  2.62 us
    pallas_call x1, Pallas kernels, on_device(): pl.pallas_call(down_kernel, out_shape=tuple((shape_of(planes, 3, h, LANES...  2.53 us
    pallas_call x1, Pallas kernels, on_device(): pl.pallas_call(pack_kernel, out_shape=(shape_of(PLANES, rows, cols),) + (...  1.12 us
  transfers between devices with their start and end apart: 6, of which 2 were waited for; matrix products, arithmetic and copies ran while one was open for 0% of the time, Pallas kernels for 0%

profile of v3, /device:TPU:0, one launch (start us, length us, event | category | flops | bytes accessed | tf_op | source)
XLA Modules:
  0.0 34.5 jit_solution(10304979482309892656)
XLA Ops:
  0.6 1.1 %pack.1 = (f32[9,32,256]{2,1,0:T(8,128)S(1)}, f32[32,256]{1,0:T(8,128)S(1)}, f32[32,256]{1,0:T(8,128)S(1)}) custom-call(f32[2,32,256]{2,1,0:T(8,128)} %source.1, f32[2,32,256]{2,1,0:T(8,128)} %coef_x.1, f32[2,32,256]{2,1,0:T(8,128)} %coef_y.1, f32[2,32,256]{2,1,0:T(8,128)} %surface.1, f32[32,256]{1,0:T(8,128)} %coef_z.1), custom_call_target="tpu_custom_call" | custom-call | tf_op jit(solution)/shard_map/pack/pallas_call | solution.py:450
  1.8 3.0 %collective-permute-start.2 = (f32[32,256]{1,0:T(8,128)S(1)}, f32[32,256]{1,0:T(8,128)S(1)}, u32[]{:S(2)}, u32[]{:S(2)}) collective-permute-start(f32[32,256]{1,0:T(8,128)S(1)} %get-tuple-element.10), channel_id=1, source_target_pairs={{0,1},{1,0},{2,3},{3,2},{4,5},{5,4},{6,7},{7,6},{8,9},{9,8},{10,11... | collective-permute-start | bytes 98312 | tf_op jit(solution)/shard_map/ppermute | solution.py:30
  4.8 1.5 %collective-permute-start.1 = (f32[9,32,256]{2,1,0:T(8,128)S(1)}, f32[9,32,256]{2,1,0:T(8,128)S(1)}, u32[]{:S(2)}, u32[]{:S(2)}) collective-permute-start(f32[9,32,256]{2,1,0:T(8,128)S(1)} %get-tuple-element.9.own_ref), channel_id=1, source_target_pairs={{0,2},{1,3},{2,0},{3,1},{4,8},{5,9},{6,10},{7,11},{8,4},{9,5},{10,... | collective-permute-start | bytes 884744 | tf_op jit(solution)/shard_map/ppermute | solution.py:40
  6.3 0.2 collective-permute-start
  6.5 1.5 %collective-permute-start.3 = (f32[32,256]{1,0:T(8,128)S(1)}, f32[32,256]{1,0:T(8,128)S(1)}, u32[]{:S(2)}, u32[]{:S(2)}) collective-permute-start(f32[32,256]{1,0:T(8,128)S(1)} %get-tuple-element.11), channel_id=1, source_target_pairs={{1,2},{2,1},{3,0},{0,3},{5,6},{6,5},{7,4},{4,7},{9,10},{10,9},{11,... | collective-permute-start | bytes 98312 | tf_op jit(solution)/shard_map/ppermute | solution.py:30
  7.9 0.0 collective-permute-done.2
  8.0 3.4 %collective-permute-done.3 = f32[32,256]{1,0:T(8,128)S(1)} collective-permute-done((f32[32,256]{1,0:T(8,128)S(1)}, f32[32,256]{1,0:T(8,128)S(1)}, u32[]{:S(2)}, u32[]{:S(2)}) %collective-permute-start.3) | collective-permute-done | bytes 32800 | tf_op jit(solution)/shard_map/ppermute | solution.py:30
  11.3 1.6 %collective-permute-start.5 = (f32[64,256]{1,0:T(8,128)S(1)}, f32[64,256]{1,0:T(8,128)S(1)}, u32[]{:S(2)}, u32[]{:S(2)}) collective-permute-start(f32[64,256]{1,0:T(8,128)S(1)} %constant_dynamic-update-slice_fusion.own_cd), channel_id=1, source_target_pairs={{0,2},{1,3},{2,0},{3,1},{4,8},{5,9},{6,10},{7,11},{8,4},{9,5},{10,... | collective-permute-start | bytes 196616 | tf_op jit(solution)/shard_map/ppermute | solution.py:40
  12.9 0.1 collective-permute-start.4
  13.0 2.6 %collective-permute-done.5.far_cd = f32[64,256]{1,0:T(8,128)S(1)} collective-permute-done((f32[64,256]{1,0:T(8,128)S(1)}, f32[64,256]{1,0:T(8,128)S(1)}, u32[]{:S(2)}, u32[]{:S(2)}) %collective-permute-start.5) | collective-permute-done | bytes 65568 | tf_op jit(solution)/shard_map/ppermute | solution.py:40
  15.6 0.0 collective-permute-done.4.near_cd
  15.6 0.0 collective-permute-done.1.far_ref
  15.6 0.0 collective-permute-done.near_ref
  15.6 2.5 %down.1 = (f32[13,3,112,128]{3,2,1,0:T(8,128)S(1)}, f32[13,3,64,128]{3,2,1,0:T(8,128)S(1)}, f32[13,3,40,128]{3,2,1,0:T(8,128)S(1)}, f32[32,1,1152]{2,1,0:T(1,128)S(1)}) custom-call(f32[9,32,256]{2,1,0:T(8,128)S(1)} %get-tuple-element.9.own_ref, f32[9,32,256]{2,1,0:T(8,128)S(1)} %collective-permute-done.near_ref, ...), custom_call_target="tpu_custom_call" | custom-call | tf_op jit(solution)/shard_map/down/pallas_call | solution.py:474
  18.1 11.7 %all_to_all.5 = f32[32,1,1152]{2,1,0:T(1,128)S(1)} all-to-all(f32[32,1,1152]{2,1,0:T(1,128)S(1)} %get-tuple-element.12), channel_id=1, replica_groups=mesh['gx'=8,'gy'=4] {'gx','gy'}, dimensions={0} | all-to-all | bytes 294912 | tf_op jit(solution)/shard_map/all_to_all | solution.py:483
  29.9 4.7 %up.1 = (f32[2,32,256]{2,1,0:T(8,128)}, f32[2,32,256]{2,1,0:T(8,128)}) custom-call(f32[288,128]{1,0:T(8,128)S(1)} %bitcast.1, f32[13,3,112,128]{3,2,1,0:T(8,128)S(1)} %get-tuple-element.13.l0, f32[13,3,64,128]{3,2,1,0:T(8,128)S(1)} %get-tuple-element.14.l1, f32[13,3,40,128]{3,2,1,0:T(8,128)S(1)} %get-tuple-element.15.l2), custom_call_target="tpu_custom_call" | custom-call | tf_op jit(solution)/shard_map/up/pallas_call | solution.py:487
  (2 shorter events, 0.0 us)
Async XLA Ops:
  1.8 6.2 %collective-permute-start.2 = (f32[32,256]{1,0:T(8,128)S(1)}, f32[32,256]{1,0:T(8,128)S(1)}, u32[]{:S(2)}, u32[]{:S(2)}) collective-permute-start(f32[32,256]{1,0:T(8,128)S(1)} %get-tuple-element.10), channel_id=1, source_target_pairs={{0,1},{1,0},{2,3},{3,2},{4,5},{5,4},{6,7},{7,6},{8,9},{9,8},{10,11... | collective-permute-start | bytes 98312 | tf_op jit(solution)/shard_map/ppermute | solution.py:30
  4.8 10.8 %collective-permute-start.1 = (f32[9,32,256]{2,1,0:T(8,128)S(1)}, f32[9,32,256]{2,1,0:T(8,128)S(1)}, u32[]{:S(2)}, u32[]{:S(2)}) collective-permute-start(f32[9,32,256]{2,1,0:T(8,128)S(1)} %get-tuple-element.9.own_ref), channel_id=1, source_target_pairs={{0,2},{1,3},{2,0},{3,1},{4,8},{5,9},{6,10},{7,11},{8,4},{9,5},{10,... | collective-permute-start | bytes 884744 | tf_op jit(solution)/shard_map/ppermute | solution.py:40
  6.3 9.3 %collective-permute-start = (f32[9,32,256]{2,1,0:T(8,128)S(1)}, f32[9,32,256]{2,1,0:T(8,128)S(1)}, u32[]{:S(2)}, u32[]{:S(2)}) collective-permute-start(f32[9,32,256]{2,1,0:T(8,128)S(1)} %get-tuple-element.9.own_ref), channel_id=1, source_target_pairs={{0,4},{4,0},{8,12},{12,8},{16,20},{20,16},{24,28},{28,24},{1,5},{5... | collective-permute-start | bytes 884744 | tf_op jit(solution)/shard_map/ppermute | solution.py:30
  6.5 4.9 %collective-permute-start.3 = (f32[32,256]{1,0:T(8,128)S(1)}, f32[32,256]{1,0:T(8,128)S(1)}, u32[]{:S(2)}, u32[]{:S(2)}) collective-permute-start(f32[32,256]{1,0:T(8,128)S(1)} %get-tuple-element.11), channel_id=1, source_target_pairs={{1,2},{2,1},{3,0},{0,3},{5,6},{6,5},{7,4},{4,7},{9,10},{10,9},{11,... | collective-permute-start | bytes 98312 | tf_op jit(solution)/shard_map/ppermute | solution.py:30
  11.3 4.3 %collective-permute-start.5 = (f32[64,256]{1,0:T(8,128)S(1)}, f32[64,256]{1,0:T(8,128)S(1)}, u32[]{:S(2)}, u32[]{:S(2)}) collective-permute-start(f32[64,256]{1,0:T(8,128)S(1)} %constant_dynamic-update-slice_fusion.own_cd), channel_id=1, source_target_pairs={{0,2},{1,3},{2,0},{3,1},{4,8},{5,9},{6,10},{7,11},{8,4},{9,5},{10,... | collective-permute-start | bytes 196616 | tf_op jit(solution)/shard_map/ppermute | solution.py:40
  12.9 2.7 %collective-permute-start.4 = (f32[64,256]{1,0:T(8,128)S(1)}, f32[64,256]{1,0:T(8,128)S(1)}, u32[]{:S(2)}, u32[]{:S(2)}) collective-permute-start(f32[64,256]{1,0:T(8,128)S(1)} %constant_dynamic-update-slice_fusion.own_cd), channel_id=1, source_target_pairs={{0,4},{4,0},{8,12},{12,8},{16,20},{20,16},{24,28},{28,24},{1,5},{5... | collective-permute-start | bytes 196616 | tf_op jit(solution)/shard_map/ppermute | solution.py:30

commit v4 on v3

--- a/solution.py
+++ b/solution.py
@@ -71,6 +71,22 @@
     out = surf * u + kx * (u - u_up) + kx_lo * (u - u_dn)
     out = out + flux - from_left(flux, step)
     return f - (out + jnp.concatenate([vert, -vert], axis=0))
+
+
+def lane_take(x, index):
+    parts = [
+        jnp.take_along_axis(x[r : r + 8], index[r : r + 8], axis=1, mode="promise_in_bounds")
+        for r in range(0, x.shape[0], 8)
+    ]
+    return parts[0] if len(parts) == 1 else jnp.concatenate(parts, axis=0)
+
+
+def row_take(x, index):
+    parts = [
+        jnp.take_along_axis(x[r : r + 8], index[r : r + 8], axis=0, mode="promise_in_bounds")
+        for r in range(0, x.shape[0], 8)
+    ]
+    return parts[0] if len(parts) == 1 else jnp.concatenate(parts, axis=0)
 
 
 def rows_of(ref, plane, count, start, size=8):
@@ -217,7 +233,7 @@
         low, high = [], []
         for a in range(2):
             held = []
-            for base in (0, rows):
+            for base in (rows, 0):
                 at = (slice(base + r0, base + r0 + 8), slice(a * LANES, (a + 1) * LANES))
                 if part == 1:
                     held.append(own_cd[at])
@@ -272,14 +288,19 @@
             put(rr, 0, r0, block_residual(level, level, U, step, r0)[1])
 
     own = l2.shape[2] // 2 - 4
-    f, kx, ky, surf_kz = coarse_block(l2, rr, 4, own, 4)
+    f, kx, ky, surf_kz = coarse_block(l2, rr, 4, own, 8)
     nine = jnp.concatenate([f, kx, ky, surf_kz], axis=0)
+    place = lax.broadcasted_iota(jnp.int32, (8, LANES), 0)
+    cell = lane % 32
+    index = cell * 8 % LANES
+    mine = place == (lane // 32 + lax.axis_index("gy")) % 4
     total = jnp.zeros((PLANES, LANES), jnp.float32)
     for r in range(4):
         for c in range(2):
             src = lax.broadcasted_iota(jnp.int32, (LANES, LANES), 0) + c * LANES
-            dst = lax.broadcasted_iota(jnp.int32, (LANES, LANES), 1) - r * 32
-            pick = jnp.where((src == dst * 8) & (dst >= 0) & (dst < 32), 1.0, 0.0)
+            dst = lax.broadcasted_iota(jnp.int32, (LANES, LANES), 1)
+            group = (dst // 32 + lax.axis_index("gy")) % 4
+            pick = jnp.where((src == dst % 32 * 8) & (group == r), 1.0, 0.0)
             total = total + jnp.dot(
                 nine[:, c, r, :],
                 pick,
@@ -293,16 +314,30 @@
         )
 
 
-def whole_sweep(level, u, weights, step):
+def scaled(level, weights, step):
+    f, kx, kx_lo, ky, kz, surf = level
+    faces = (f, kx, kx_lo, ky, from_left(ky, step), kz)
+    return tuple(weights * x for x in faces)
+
+
+def whole_sweep(faces, u, step):
+    f, up, down, right, left, across = faces
+    rows = u.shape[2]
+    other = jnp.concatenate([u[1:2], u[0:1]], axis=0)
+    near = ((1.0 - damping) * u + f) + across * other
+    along = up * pltpu.roll(u, rows - 1, 2) + down * pltpu.roll(u, 1, 2)
+    return near + along + (right * from_right(u, step) + left * from_left(u, step))
+
+
+def whole_residual(level, u, step):
     f, kx, kx_lo, ky, kz, surf = level
     rows = u.shape[2]
-    r = residual_of(
+    return residual_of(
         f, u, pltpu.roll(u, rows - 1, 2), pltpu.roll(u, 1, 2), kx, kx_lo, ky, kz, surf, step
     )
-    return u + weights * r, r
-
-
-def up_kernel(nx, ny, x_ref, l0, l1, l2, p_ref, r_ref, g3, g4, ub, uc):
+
+
+def up_kernel(nx, ny, x_ref, l0, l1, l2, p_ref, r_ref, g3, g4, g5, ub, uc):
     me_x = lax.axis_index("gx")
     me_y = lax.axis_index("gy")
     tiles = ny // 4
@@ -310,6 +345,8 @@
 
     lane = lane_iota((rows3, LANES))
     row = lax.broadcasted_iota(jnp.int32, (rows3, LANES), 0)
+    to_row = row % 8 // 4 * 4 + (row - lane // 32 + 4) % 4
+    to_lane = (row - lane // 32 + 4) % 4 * 32 + lane % 32
     for p in range(PLANES):
         for q in range(tiles):
             if tiles == 1:
@@ -322,13 +359,7 @@
                     ],
                     axis=0,
                 )
-            out = x
-            for delta in range(-3, 4):
-                if delta == 0:
-                    continue
-                moved = pltpu.roll(x, (-delta) % rows3, 0)
-                moved = pltpu.roll(moved, (32 * delta) % LANES, 1)
-                out = jnp.where(lane // 32 - row % 4 == delta, moved, out)
+            out = lane_take(row_take(x, to_row), to_lane)
             g3[p, q, :, :] = out
 
     def gathered(ref):
@@ -344,17 +375,17 @@
 
     level3 = gathered(g3)
     w3 = weight(*level3[1:], 1)
-    u3 = w3 * level3[0]
-    u3, unused = whole_sweep(level3, u3, w3, 1)
-    unused, r3 = whole_sweep(level3, u3, w3, 1)
-    g4[0:2] = r3
+    faces3 = scaled(level3, w3, 1)
+    u3 = whole_sweep(faces3, faces3[0], 1)
+    g4[0:2] = whole_residual(level3, u3, 1)
     f, kx, ky, surf_kz = coarse_block(g3, g4, 1, 0, rows3 // 2)
     level4 = (f, kx, pltpu.roll(kx, 1, 2), ky, surf_kz[2:3], surf_kz[0:2])
     w4 = weight(*level4[1:], 2)
-    u4 = w4 * f
-    for step in range(CSWEEPS - 1):
-        u4, unused = whole_sweep(level4, u4, w4, 2)
-    unused, rc = whole_sweep(level4, u4, w4, 2)
+    faces4 = scaled(level4, w4, 2)
+    u4 = faces4[0]
+    for sweep in range(CSWEEPS - 1):
+        u4 = whole_sweep(faces4, u4, 2)
+    rc = whole_residual(level4, u4, 2)
     even = lane_iota(u4.shape) % 2 == 0
 
     def total(x):
@@ -366,31 +397,32 @@
     put_strided(g4, 0, 0, e4)
     put_strided(g4, 0, 1, e4)
     u3 = u3 + g4[0:2]
-    for step in range(POST):
-        u3, unused = whole_sweep(level3, u3, w3, 1)
+    for sweep in range(POST):
+        u3 = whole_sweep(faces3, u3, 1)
 
     rows2 = l2.shape[2] - 2 * PAD
-    to_row = lax.broadcasted_iota(jnp.int32, (rows2, rows3), 0) // 2 - 4 + me_x * 4
-    pick_row = jnp.where(
-        to_row == lax.broadcasted_iota(jnp.int32, (rows2, rows3), 1), 1.0, 0.0
-    )
-    dot = functools.partial(
-        jnp.dot, precision=lax.Precision.HIGHEST, preferred_element_type=jnp.float32
-    )
-    near = [[dot(pick_row, u3[k, q]) for q in range(tiles)] for k in range(2)]
-    near = [jnp.concatenate([near[k][q] for k in range(2)], axis=0) for q in range(tiles)]
-    for c in range(3):
-        spread = jnp.zeros((2 * rows2, LANES), jnp.float32)
-        for q in range(tiles):
-            column = lax.broadcasted_iota(jnp.int32, (LANES, LANES), 1) + c * LANES
+    margin = jnp.zeros((2, tiles, PAD, LANES), jnp.float32)
+    g5[:, :, 0:PAD] = margin
+    g5[:, :, PAD : PAD + rows3] = u3
+    g5[:, :, PAD + rows3 : 2 * PAD + rows3] = margin
+    lane = lane_iota((8, LANES))
+    first = me_x * 4 + PAD - 2
+    skip = rows2 // 2 - 8
+    for k in range(2):
+        near = [g5[k, q, pl.ds(first, 8), :] for q in range(tiles)]
+        for c in range(3):
+            column = lane + c * LANES
             column = jnp.where(column >= 320, column - 384, column)
-            coarse = (column + 64) // 8 - 8 + me_y * 32 - q * LANES
-            pick = jnp.where(
-                coarse == lax.broadcasted_iota(jnp.int32, (LANES, LANES), 0), 1.0, 0.0
-            )
-            spread = spread + dot(near[q], pick)
-        for k in range(2):
-            uc[k, c, PAD : PAD + rows2, :] = spread[k * rows2 : (k + 1) * rows2]
+            coarse = (column + 64) // 8 - 8 + me_y * 32 + LANES
+            index = coarse % LANES
+            spread = lane_take(near[0], index)
+            for q in range(1, tiles):
+                spread = jnp.where(coarse // LANES == q + 1, lane_take(near[q], index), spread)
+            zero = jnp.zeros((skip, LANES), jnp.float32)
+            uc[k, c, PAD : PAD + skip, :] = zero
+            uc[k, c, PAD + rows2 - skip : PAD + rows2, :] = zero
+            for at in (PAD + skip, PAD + skip + 1):
+                uc[k, c, pl.ds(at, 8, stride=2), :] = spread
 
     levels = (l0, l1, l2)
     zeros = jnp.zeros((2, 3, PAD, LANES), jnp.float32)
@@ -465,7 +497,7 @@
     strip_d = pair_permute(strip_d, "gy", 1, wrap=True)
     far = far_permute(packed)
     near = pair_permute(packed, "gx", 0)
-    strips = jnp.concatenate([strip_c, strip_d], axis=0)
+    strips = jnp.concatenate([strip_d, strip_c], axis=0)
     far_strips = far_permute(strips)
     near_strips = pair_permute(strips, "gx", 0)
 
@@ -490,6 +522,7 @@
         scratch_shapes=[
             vmem(PLANES, tiles, nx * 4, LANES),
             vmem(2, tiles, nx * 4, LANES),
+            vmem(2, tiles, nx * 4 + 2 * PAD, LANES),
             vmem(2, 3, heights[0], LANES),
             vmem(2, 3, heights[0], LANES),
         ],

time: 34.7 us -> 32.8 us (0.945)
  Pallas kernels: 8.33 us -> 7.23 us
  blocking collectives: 11.7 us -> 10.9 us
    ppermute x4, starting transfers between devices: 4.73 us -> 6.87 us  [pair_permute(): return lax.ppermute(x, axis, pairs)]
    ppermute x2, starting transfers between devices: 3.1 us -> 1.01 us  [far_permute(): return lax.ppermute(x, ('gx', 'gy'), pairs)]
    pallas_call x1, Pallas kernels: 4.68 us -> 3.54 us  [on_device(): pl.pallas_call(functools.partial(up_kernel, nx, ny), out_shape=(shape_of(...]
    all_to_all x1, blocking collectives: 11.7 us -> 10.9 us  [on_device(): everyone = lax.all_to_all(pack, ('gx', 'gy'), 0, 0, tiled=True)]
where the time goes in v4:
time: 32.8 us; the launch traced here: 32.6 us
  blocking collectives  10.9 us (33%)
  starting transfers between devices  7.88 us (24%)
  Pallas kernels  7.23 us (22%)
  waiting for transfers between devices  5.96 us (18%)
  between operations  0.66 us (2%)
    all_to_all x1, blocking collectives, on_device(): everyone = lax.all_to_all(pack, ('gx', 'gy'), 0, 0, tiled=True)  10.9 us
    ppermute x4, starting transfers between devices, pair_permute(): return lax.ppermute(x, axis, pairs)  6.87 us
    pallas_call x1, Pallas kernels, on_device(): pl.pallas_call(functools.partial(up_kernel, nx, ny), out_shape=(shape_of(...  3.54 us
    ppermute x4, waiting for transfers between devices, pair_permute(): return lax.ppermute(x, axis, pairs)  3.38 us
    ppermute x2, waiting for transfers between devices, far_permute(): return lax.ppermute(x, ('gx', 'gy'), pairs)  2.58 us
    pallas_call x1, Pallas kernels, on_device(): pl.pallas_call(down_kernel, out_shape=tuple((shape_of(planes, 3, h, LANES...  2.57 us
    pallas_call x1, Pallas kernels, on_device(): pl.pallas_call(pack_kernel, out_shape=(shape_of(PLANES, rows, cols),) + (...  1.12 us
    ppermute x2, starting transfers between devices, far_permute(): return lax.ppermute(x, ('gx', 'gy'), pairs)  1.01 us
  transfers between devices with their start and end apart: 6, of which 2 were waited for; matrix products, arithmetic and copies ran while one was open for 0% of the time, Pallas kernels for 0%

profile of v4, /device:TPU:0, one launch (start us, length us, event | category | flops | bytes accessed | tf_op | source)
XLA Modules:
  0.0 32.6 jit_solution(1580277995491038998)
XLA Ops:
  0.6 1.1 %pack.1 = (f32[9,32,256]{2,1,0:T(8,128)S(1)}, f32[32,256]{1,0:T(8,128)S(1)}, f32[32,256]{1,0:T(8,128)S(1)}) custom-call(f32[2,32,256]{2,1,0:T(8,128)} %source.1, f32[2,32,256]{2,1,0:T(8,128)} %coef_x.1, f32[2,32,256]{2,1,0:T(8,128)} %coef_y.1, f32[2,32,256]{2,1,0:T(8,128)} %surface.1, f32[32,256]{1,0:T(8,128)} %coef_z.1), custom_call_target="tpu_custom_call" | custom-call | tf_op jit(solution)/shard_map/pack/pallas_call | solution.py:482
  1.8 4.0 %collective-permute-start.2 = (f32[32,256]{1,0:T(8,128)S(1)}, f32[32,256]{1,0:T(8,128)S(1)}, u32[]{:S(2)}, u32[]{:S(2)}) collective-permute-start(f32[32,256]{1,0:T(8,128)S(1)} %get-tuple-element.10), channel_id=1, source_target_pairs={{1,2},{2,1},{3,0},{0,3},{5,6},{6,5},{7,4},{4,7},{9,10},{10,9},{11,... | collective-permute-start | bytes 98312 | tf_op jit(solution)/shard_map/ppermute | solution.py:30
  5.7 0.5 %collective-permute-start.1 = (f32[9,32,256]{2,1,0:T(8,128)S(1)}, f32[9,32,256]{2,1,0:T(8,128)S(1)}, u32[]{:S(2)}, u32[]{:S(2)}) collective-permute-start(f32[9,32,256]{2,1,0:T(8,128)S(1)} %get-tuple-element.9.own_ref), channel_id=1, source_target_pairs={{0,2},{1,3},{2,0},{3,1},{4,8},{5,9},{6,10},{7,11},{8,4},{9,5},{10,... | collective-permute-start | bytes 884744 | tf_op jit(solution)/shard_map/ppermute | solution.py:40
  6.2 1.2 %collective-permute-start = (f32[9,32,256]{2,1,0:T(8,128)S(1)}, f32[9,32,256]{2,1,0:T(8,128)S(1)}, u32[]{:S(2)}, u32[]{:S(2)}) collective-permute-start(f32[9,32,256]{2,1,0:T(8,128)S(1)} %get-tuple-element.9.own_ref), channel_id=1, source_target_pairs={{0,4},{4,0},{8,12},{12,8},{16,20},{20,16},{24,28},{28,24},{1,5},{5... | collective-permute-start | bytes 884744 | tf_op jit(solution)/shard_map/ppermute | solution.py:30
  7.4 0.5 %collective-permute-start.3 = (f32[32,256]{1,0:T(8,128)S(1)}, f32[32,256]{1,0:T(8,128)S(1)}, u32[]{:S(2)}, u32[]{:S(2)}) collective-permute-start(f32[32,256]{1,0:T(8,128)S(1)} %get-tuple-element.11), channel_id=1, source_target_pairs={{0,1},{1,0},{2,3},{3,2},{4,5},{5,4},{6,7},{7,6},{8,9},{9,8},{10,11... | collective-permute-start | bytes 98312 | tf_op jit(solution)/shard_map/ppermute | solution.py:30
  7.9 0.0 collective-permute-done.2
  8.0 3.4 %collective-permute-done.3 = f32[32,256]{1,0:T(8,128)S(1)} collective-permute-done((f32[32,256]{1,0:T(8,128)S(1)}, f32[32,256]{1,0:T(8,128)S(1)}, u32[]{:S(2)}, u32[]{:S(2)}) %collective-permute-start.3) | collective-permute-done | bytes 32800 | tf_op jit(solution)/shard_map/ppermute | solution.py:30
  11.3 0.5 %collective-permute-start.5 = (f32[64,256]{1,0:T(8,128)S(1)}, f32[64,256]{1,0:T(8,128)S(1)}, u32[]{:S(2)}, u32[]{:S(2)}) collective-permute-start(f32[64,256]{1,0:T(8,128)S(1)} %constant_dynamic-update-slice_fusion.own_cd), channel_id=1, source_target_pairs={{0,2},{1,3},{2,0},{3,1},{4,8},{5,9},{6,10},{7,11},{8,4},{9,5},{10,... | collective-permute-start | bytes 196616 | tf_op jit(solution)/shard_map/ppermute | solution.py:40
  11.8 1.2 %collective-permute-start.4 = (f32[64,256]{1,0:T(8,128)S(1)}, f32[64,256]{1,0:T(8,128)S(1)}, u32[]{:S(2)}, u32[]{:S(2)}) collective-permute-start(f32[64,256]{1,0:T(8,128)S(1)} %constant_dynamic-update-slice_fusion.own_cd), channel_id=1, source_target_pairs={{0,4},{4,0},{8,12},{12,8},{16,20},{20,16},{24,28},{28,24},{1,5},{5... | collective-permute-start | bytes 196616 | tf_op jit(solution)/shard_map/ppermute | solution.py:30
  13.0 2.6 %collective-permute-done.5.far_cd = f32[64,256]{1,0:T(8,128)S(1)} collective-permute-done((f32[64,256]{1,0:T(8,128)S(1)}, f32[64,256]{1,0:T(8,128)S(1)}, u32[]{:S(2)}, u32[]{:S(2)}) %collective-permute-start.5) | collective-permute-done | bytes 65568 | tf_op jit(solution)/shard_map/ppermute | solution.py:40
  15.6 0.0 collective-permute-done.4.near_cd
  15.6 0.0 collective-permute-done.1.far_ref
  15.6 0.0 collective-permute-done.near_ref
  15.6 2.6 %down.1 = (f32[13,3,112,128]{3,2,1,0:T(8,128)S(1)}, f32[13,3,64,128]{3,2,1,0:T(8,128)S(1)}, f32[13,3,40,128]{3,2,1,0:T(8,128)S(1)}, f32[32,1,1152]{2,1,0:T(1,128)S(1)}) custom-call(f32[9,32,256]{2,1,0:T(8,128)S(1)} %get-tuple-element.9.own_ref, f32[9,32,256]{2,1,0:T(8,128)S(1)} %collective-permute-done.near_ref, ...), custom_call_target="tpu_custom_call" | custom-call | tf_op jit(solution)/shard_map/down/pallas_call | solution.py:506
  18.2 10.9 %all_to_all.5 = f32[32,1,1152]{2,1,0:T(1,128)S(1)} all-to-all(f32[32,1,1152]{2,1,0:T(1,128)S(1)} %get-tuple-element.12), channel_id=1, replica_groups=mesh['gx'=8,'gy'=4] {'gx','gy'}, dimensions={0} | all-to-all | bytes 294912 | tf_op jit(solution)/shard_map/all_to_all | solution.py:515
  29.1 3.5 %up.1 = (f32[2,32,256]{2,1,0:T(8,128)}, f32[2,32,256]{2,1,0:T(8,128)}) custom-call(f32[288,128]{1,0:T(8,128)S(1)} %bitcast.1, f32[13,3,112,128]{3,2,1,0:T(8,128)S(1)} %get-tuple-element.13.l0, f32[13,3,64,128]{3,2,1,0:T(8,128)S(1)} %get-tuple-element.14.l1, f32[13,3,40,128]{3,2,1,0:T(8,128)S(1)} %get-tuple-element.15.l2), custom_call_target="tpu_custom_call" | custom-call | tf_op jit(solution)/shard_map/up/pallas_call | solution.py:519
  (2 shorter events, 0.0 us)
Async XLA Ops:
  1.8 6.2 %collective-permute-start.2 = (f32[32,256]{1,0:T(8,128)S(1)}, f32[32,256]{1,0:T(8,128)S(1)}, u32[]{:S(2)}, u32[]{:S(2)}) collective-permute-start(f32[32,256]{1,0:T(8,128)S(1)} %get-tuple-element.10), channel_id=1, source_target_pairs={{1,2},{2,1},{3,0},{0,3},{5,6},{6,5},{7,4},{4,7},{9,10},{10,9},{11,... | collective-permute-start | bytes 98312 | tf_op jit(solution)/shard_map/ppermute | solution.py:30
  5.7 9.9 %collective-permute-start.1 = (f32[9,32,256]{2,1,0:T(8,128)S(1)}, f32[9,32,256]{2,1,0:T(8,128)S(1)}, u32[]{:S(2)}, u32[]{:S(2)}) collective-permute-start(f32[9,32,256]{2,1,0:T(8,128)S(1)} %get-tuple-element.9.own_ref), channel_id=1, source_target_pairs={{0,2},{1,3},{2,0},{3,1},{4,8},{5,9},{6,10},{7,11},{8,4},{9,5},{10,... | collective-permute-start | bytes 884744 | tf_op jit(solution)/shard_map/ppermute | solution.py:40
  6.2 9.4 %collective-permute-start = (f32[9,32,256]{2,1,0:T(8,128)S(1)}, f32[9,32,256]{2,1,0:T(8,128)S(1)}, u32[]{:S(2)}, u32[]{:S(2)}) collective-permute-start(f32[9,32,256]{2,1,0:T(8,128)S(1)} %get-tuple-element.9.own_ref), channel_id=1, source_target_pairs={{0,4},{4,0},{8,12},{12,8},{16,20},{20,16},{24,28},{28,24},{1,5},{5... | collective-permute-start | bytes 884744 | tf_op jit(solution)/shard_map/ppermute | solution.py:30
  7.4 3.9 %collective-permute-start.3 = (f32[32,256]{1,0:T(8,128)S(1)}, f32[32,256]{1,0:T(8,128)S(1)}, u32[]{:S(2)}, u32[]{:S(2)}) collective-permute-start(f32[32,256]{1,0:T(8,128)S(1)} %get-tuple-element.11), channel_id=1, source_target_pairs={{0,1},{1,0},{2,3},{3,2},{4,5},{5,4},{6,7},{7,6},{8,9},{9,8},{10,11... | collective-permute-start | bytes 98312 | tf_op jit(solution)/shard_map/ppermute | solution.py:30
  11.3 4.3 %collective-permute-start.5 = (f32[64,256]{1,0:T(8,128)S(1)}, f32[64,256]{1,0:T(8,128)S(1)}, u32[]{:S(2)}, u32[]{:S(2)}) collective-permute-start(f32[64,256]{1,0:T(8,128)S(1)} %constant_dynamic-update-slice_fusion.own_cd), channel_id=1, source_target_pairs={{0,2},{1,3},{2,0},{3,1},{4,8},{5,9},{6,10},{7,11},{8,4},{9,5},{10,... | collective-permute-start | bytes 196616 | tf_op jit(solution)/shard_map/ppermute | solution.py:40
  11.8 3.8 %collective-permute-start.4 = (f32[64,256]{1,0:T(8,128)S(1)}, f32[64,256]{1,0:T(8,128)S(1)}, u32[]{:S(2)}, u32[]{:S(2)}) collective-permute-start(f32[64,256]{1,0:T(8,128)S(1)} %constant_dynamic-update-slice_fusion.own_cd), channel_id=1, source_target_pairs={{0,4},{4,0},{8,12},{12,8},{16,20},{20,16},{24,28},{28,24},{1,5},{5... | collective-permute-start | bytes 196616 | tf_op jit(solution)/shard_map/ppermute | solution.py:30

commit v5 on v4

--- a/solution.py
+++ b/solution.py
@@ -129,14 +129,6 @@
             ref[plane + p, c, pl.ds(start, value.shape[2], stride=2), :] = value[p, c]
 
 
-def zero_pads(ref, planes):
-    rows = ref.shape[2]
-    for plane in planes:
-        zero = jnp.zeros((1, ref.shape[1], PAD, LANES), jnp.float32)
-        put(ref, plane, 0, zero)
-        put(ref, plane, rows - PAD, zero)
-
-
 def coarse_block(fine, resid, step, fine_row, size):
     def both(ref, plane, count):
         return strided(ref, plane, count, fine_row, size) + strided(
@@ -150,6 +142,11 @@
     summed = jnp.concatenate([f, kx, surf_kz], axis=0)
     summed = summed + from_right(summed, step)
     return summed[0:2], summed[2:4], from_right(ky, step), summed[4:7]
+
+
+def blocks(own, count, halo):
+    more = -(-halo // 8) * 8
+    return range(own - more, own + count + more, 8)
 
 
 def sides(mine, other, is_even):
@@ -206,7 +203,7 @@
 
 
 def down_kernel(
-    own_ref, near_ref, far_ref, own_cd, near_cd, far_cd, l0, l1, l2, pack_ref, ua, rr
+    own_ref, near_ref, far_ref, own_cd, near_cd, far_cd, l0, l1, l2, pack_ref, ua, rr, row9
 ):
     even_y = lax.rem(lax.axis_index("gy"), 2) == 0
     rows = own_ref.shape[1]
@@ -249,18 +246,14 @@
                 lane < WIDTH, right, jnp.where(lane >= LANES - WIDTH, left, 0.0)
             )
 
-    for ref in (l0, l1, l2):
-        zero_pads(ref, (KX, KX + 1, U, U + 1))
-    for ref in (ua,):
-        zero_pads(ref, (0, 1))
-
+    halos = ((26, 25, 24), (12, 11, 10), (5, 4, 0))
     levels = (l0, l1, l2)
     for depth, level in enumerate(levels):
         step = 1 << depth
-        count = level.shape[2] - 2 * PAD
-        starts = range(PAD, PAD + count, 8)
+        count = (level.shape[2] - 2 * PAD) // 3
+        first, second, last = (blocks(PAD + count, count, halo) for halo in halos[depth])
         if depth:
-            for r0 in starts:
+            for r0 in range(PAD, PAD + 3 * count, 8):
                 f, kx, ky, surf_kz = coarse_block(
                     levels[depth - 1], rr, step // 2, PAD + 2 * (r0 - PAD), 8
                 )
@@ -268,9 +261,7 @@
                 put(level, KX, r0, kx)
                 put(level, KY, r0, ky)
                 put(level, S, r0, surf_kz)
-            if count * 2 + 2 * PAD > 0:
-                put(ua, 0, PAD + count, jnp.zeros((2, 3, PAD, LANES), jnp.float32))
-        for r0 in starts:
+        for r0 in first:
             w = weight(
                 rows_of(level, KX, 2, r0),
                 rows_of(level, KX, 2, r0 - 1),
@@ -281,10 +272,10 @@
             )
             put(level, W, r0, w)
             put(ua, 0, r0, w * rows_of(level, F, 2, r0))
-        for r0 in starts:
+        for r0 in second:
             u, r = block_residual(level, ua, 0, step, r0)
             put(level, U, r0, u + rows_of(level, W, 2, r0) * r)
-        for r0 in starts:
+        for r0 in last:
             put(rr, 0, r0, block_residual(level, level, U, step, r0)[1])
 
     own = l2.shape[2] // 2 - 4
@@ -307,11 +298,10 @@
                 precision=lax.Precision.HIGHEST,
                 preferred_element_type=jnp.float32,
             )
-    for p in range(PLANES):
-        at = slice(p * LANES, (p + 1) * LANES)
-        pack_ref[:, :, at] = jnp.broadcast_to(
-            total[p : p + 1][None], (pack_ref.shape[0], 1, LANES)
-        )
+    row9[0:PLANES] = total
+    row9[PLANES : 2 * PLANES] = total
+    for r0 in range(0, pack_ref.shape[0], 8):
+        pack_ref[r0 : r0 + 8] = row9[r0 % PLANES : r0 % PLANES + 8]
 
 
 def scaled(level, weights, step):
@@ -337,7 +327,7 @@
     )
 
 
-def up_kernel(nx, ny, x_ref, l0, l1, l2, p_ref, r_ref, g3, g4, g5, ub, uc):
+def up_kernel(nx, ny, x_ref, l0, l1, l2, p_ref, r_ref, g3, g4, g5, ub, uc, p_own, r_own, sems):
     me_x = lax.axis_index("gx")
     me_y = lax.axis_index("gy")
     tiles = ny // 4
@@ -392,11 +382,11 @@
         x = jnp.sum(jnp.where(even, x, 0.0), axis=(0, 1))
         return jnp.sum(jnp.sum(x, axis=0, keepdims=True), axis=1, keepdims=True)
 
-    e4 = u4 + (total(rc) / total(level4[5]))[None, None]
-    e4 = jnp.where(even, e4, from_left(e4, 1))
-    put_strided(g4, 0, 0, e4)
-    put_strided(g4, 0, 1, e4)
-    u3 = u3 + g4[0:2]
+    shift = (total(rc) / total(level4[5]))[None, None]
+    spread4 = jnp.where(even, u4, from_left(u4, 1))
+    put_strided(g4, 0, 0, spread4)
+    put_strided(g4, 0, 1, spread4)
+    u3 = (u3 + g4[0:2]) + shift
     for sweep in range(POST):
         u3 = whole_sweep(faces3, u3, 1)
 
@@ -418,53 +408,51 @@
             spread = lane_take(near[0], index)
             for q in range(1, tiles):
                 spread = jnp.where(coarse // LANES == q + 1, lane_take(near[q], index), spread)
-            zero = jnp.zeros((skip, LANES), jnp.float32)
-            uc[k, c, PAD : PAD + skip, :] = zero
-            uc[k, c, PAD + rows2 - skip : PAD + rows2, :] = zero
             for at in (PAD + skip, PAD + skip + 1):
                 uc[k, c, pl.ds(at, 8, stride=2), :] = spread
 
     levels = (l0, l1, l2)
-    zeros = jnp.zeros((2, 3, PAD, LANES), jnp.float32)
     for depth in (2, 1, 0):
         level = levels[depth]
         step = 1 << depth
-        count = level.shape[2] - 2 * PAD
-        margin = (24, 8, 0)[depth]
-        starts = range(PAD + margin, PAD + count - margin, 8)
+        count = (level.shape[2] - 2 * PAD) // 3
+        own = PAD + count
+        starts = blocks(own, count, 4)
         for r0 in starts:
             put(uc, 0, r0, rows_of(uc, 0, 2, r0) + rows_of(level, U, 2, r0))
-        for buf in (uc, ub):
-            put(buf, 0, PAD + margin - 8, zeros)
-            put(buf, 0, PAD + count - margin, zeros)
         for source, target in ((uc, ub), (ub, uc)):
             for r0 in starts:
                 u, r = block_residual(level, source, 0, step, r0)
                 put(target, 0, r0, u + rows_of(level, W, 2, r0) * r)
         if depth:
-            finer = levels[depth - 1]
-            need = (24, 8, 0)[depth - 1]
             half = step // 2
-            first, last = need // 2, (finer.shape[2] - 2 * PAD - need) // 2
-            blocks = []
-            for r0 in range(first, last, 4):
-                e = rows_of(uc, 0, 2, PAD + r0, 4)
-                blocks.append(
+            finer = PAD + 2 * count - 4
+            spread = []
+            for r0 in range(own - 2, own + count + 2, 4):
+                e = rows_of(uc, 0, 2, r0, 4)
+                spread.append(
                     jnp.where(lane_iota(e.shape) % step < half, e, from_left(e, half))
                 )
-            for r0, e in zip(range(first, last, 4), blocks):
-                put_strided(ub, 0, PAD + 2 * r0, e)
-                put_strided(ub, 0, PAD + 2 * r0 + 1, e)
-            for r0 in range(PAD + need, PAD + 2 * last, 8):
-                put(uc, 0, r0, rows_of(ub, 0, 2, r0))
+            for k, e in enumerate(spread):
+                put_strided(ub, 0, finer + 8 * k, e)
+                put_strided(ub, 0, finer + 8 * k + 1, e)
+            for k in range(len(spread)):
+                put(uc, 0, finer + 8 * k, rows_of(ub, 0, 2, finer + 8 * k))
         else:
-            own = p_ref.shape[1]
-            for r0 in range(0, own, 8):
-                at = PAD + count // 2 - own // 2 + r0
-                u, r = block_residual(level, uc, 0, step, at)
+            for r0 in range(0, count, 8):
+                u = rows_of(uc, 0, 2, own + r0)
                 for c in range(2):
-                    p_ref[:, r0 : r0 + 8, c * LANES : (c + 1) * LANES] = u[:, c]
-                    r_ref[:, r0 : r0 + 8, c * LANES : (c + 1) * LANES] = r[:, c]
+                    p_own[:, r0 : r0 + 8, c * LANES : (c + 1) * LANES] = u[:, c]
+            copy_p = pltpu.make_async_copy(p_own, p_ref, sems.at[0])
+            copy_p.start()
+            for r0 in range(0, count, 8):
+                r = block_residual(level, uc, 0, step, own + r0)[1]
+                for c in range(2):
+                    r_own[:, r0 : r0 + 8, c * LANES : (c + 1) * LANES] = r[:, c]
+            copy_r = pltpu.make_async_copy(r_own, r_ref, sems.at[1])
+            copy_r.start()
+            copy_p.wait()
+            copy_r.wait()
 
 
 def shape_of(*shape):
@@ -506,13 +494,15 @@
     l0, l1, l2, pack = pl.pallas_call(
         down_kernel,
         out_shape=tuple(shape_of(planes, 3, h, LANES) for h in heights)
-        + (shape_of(nx * ny, 1, PACK),),
-        scratch_shapes=[vmem(2, 3, heights[0], LANES)] * 2,
+        + (shape_of(nx * ny * PLANES, LANES),),
+        scratch_shapes=[vmem(2, 3, heights[0], LANES)] * 2 + [vmem(24, LANES)],
         compiler_params=params,
         name="down",
     )(packed, near, far, strips, near_strips, far_strips)
 
-    everyone = lax.all_to_all(pack, ("gx", "gy"), 0, 0, tiled=True)
+    everyone = lax.all_to_all(
+        pack.reshape(nx * ny, 1, PACK), ("gx", "gy"), 0, 0, tiled=True
+    )
     everyone = everyone.reshape(nx * ny * PLANES, LANES)
 
     tiles = ny // 4
@@ -525,7 +515,11 @@
             vmem(2, tiles, nx * 4 + 2 * PAD, LANES),
             vmem(2, 3, heights[0], LANES),
             vmem(2, 3, heights[0], LANES),
+            vmem(*source.shape),
+            vmem(*source.shape),
+            pltpu.SemaphoreType.DMA((2,)),
         ],
+        out_specs=[pl.BlockSpec(memory_space=pltpu.HBM)] * 2,
         compiler_params=params,
         name="up",
     )(everyone, l0, l1, l2)

time: 32.8 us -> 32.6 us (level)
  no operation moved by 1% of the time
where the time goes in v5:
time: 32.6 us; the launch traced here: 32.4 us
  blocking collectives  10.9 us (33%)
  starting transfers between devices  7.88 us (24%)
  Pallas kernels  7.03 us (22%)
  waiting for transfers between devices  5.96 us (18%)
  between operations  0.66 us (2%)
    all_to_all x1, blocking collectives, on_device(): lax.all_to_all(pack.reshape(nx * ny, 1, PACK), ('gx', 'gy'), 0, 0, tiled=...  10.9 us
    ppermute x4, starting transfers between devices, pair_permute(): return lax.ppermute(x, axis, pairs)  6.87 us
    pallas_call x1, Pallas kernels, on_device(): pl.pallas_call(functools.partial(up_kernel, nx, ny), out_shape=(shape_of(...  3.48 us
    ppermute x4, waiting for transfers between devices, pair_permute(): return lax.ppermute(x, axis, pairs)  3.38 us
    ppermute x2, waiting for transfers between devices, far_permute(): return lax.ppermute(x, ('gx', 'gy'), pairs)  2.58 us
    pallas_call x1, Pallas kernels, on_device(): pl.pallas_call(down_kernel, out_shape=tuple((shape_of(planes, 3, h, LANES...  2.43 us
    pallas_call x1, Pallas kernels, on_device(): pl.pallas_call(pack_kernel, out_shape=(shape_of(PLANES, rows, cols),) + (...  1.12 us
    ppermute x2, starting transfers between devices, far_permute(): return lax.ppermute(x, ('gx', 'gy'), pairs)  1.01 us
  transfers between devices with their start and end apart: 6, of which 2 were waited for; matrix products, arithmetic and copies ran while one was open for 0% of the time, Pallas kernels for 0%

profile of v5, /device:TPU:0, one launch (start us, length us, event | category | flops | bytes accessed | tf_op | source)
XLA Modules:
  0.0 32.4 jit_solution(10355179777229885413)
XLA Ops:
  0.6 1.1 %pack.1 = (f32[9,32,256]{2,1,0:T(8,128)S(1)}, f32[32,256]{1,0:T(8,128)S(1)}, f32[32,256]{1,0:T(8,128)S(1)}) custom-call(f32[2,32,256]{2,1,0:T(8,128)} %source.1, f32[2,32,256]{2,1,0:T(8,128)} %coef_x.1, f32[2,32,256]{2,1,0:T(8,128)} %coef_y.1, f32[2,32,256]{2,1,0:T(8,128)} %surface.1, f32[32,256]{1,0:T(8,128)} %coef_z.1), custom_call_target="tpu_custom_call" | custom-call | tf_op jit(solution)/shard_map/pack/pallas_call | solution.py:470
  1.8 4.0 %collective-permute-start.2 = (f32[32,256]{1,0:T(8,128)S(1)}, f32[32,256]{1,0:T(8,128)S(1)}, u32[]{:S(2)}, u32[]{:S(2)}) collective-permute-start(f32[32,256]{1,0:T(8,128)S(1)} %get-tuple-element.10), channel_id=1, source_target_pairs={{1,2},{2,1},{3,0},{0,3},{5,6},{6,5},{7,4},{4,7},{9,10},{10,9},{11,... | collective-permute-start | bytes 98312 | tf_op jit(solution)/shard_map/ppermute | solution.py:30
  5.7 0.5 %collective-permute-start.1 = (f32[9,32,256]{2,1,0:T(8,128)S(1)}, f32[9,32,256]{2,1,0:T(8,128)S(1)}, u32[]{:S(2)}, u32[]{:S(2)}) collective-permute-start(f32[9,32,256]{2,1,0:T(8,128)S(1)} %get-tuple-element.9.own_ref), channel_id=1, source_target_pairs={{0,2},{1,3},{2,0},{3,1},{4,8},{5,9},{6,10},{7,11},{8,4},{9,5},{10,... | collective-permute-start | bytes 884744 | tf_op jit(solution)/shard_map/ppermute | solution.py:40
  6.2 1.2 %collective-permute-start = (f32[9,32,256]{2,1,0:T(8,128)S(1)}, f32[9,32,256]{2,1,0:T(8,128)S(1)}, u32[]{:S(2)}, u32[]{:S(2)}) collective-permute-start(f32[9,32,256]{2,1,0:T(8,128)S(1)} %get-tuple-element.9.own_ref), channel_id=1, source_target_pairs={{0,4},{4,0},{8,12},{12,8},{16,20},{20,16},{24,28},{28,24},{1,5},{5... | collective-permute-start | bytes 884744 | tf_op jit(solution)/shard_map/ppermute | solution.py:30
  7.4 0.5 %collective-permute-start.3 = (f32[32,256]{1,0:T(8,128)S(1)}, f32[32,256]{1,0:T(8,128)S(1)}, u32[]{:S(2)}, u32[]{:S(2)}) collective-permute-start(f32[32,256]{1,0:T(8,128)S(1)} %get-tuple-element.11), channel_id=1, source_target_pairs={{0,1},{1,0},{2,3},{3,2},{4,5},{5,4},{6,7},{7,6},{8,9},{9,8},{10,11... | collective-permute-start | bytes 98312 | tf_op jit(solution)/shard_map/ppermute | solution.py:30
  7.9 0.0 collective-permute-done.2
  8.0 3.4 %collective-permute-done.3 = f32[32,256]{1,0:T(8,128)S(1)} collective-permute-done((f32[32,256]{1,0:T(8,128)S(1)}, f32[32,256]{1,0:T(8,128)S(1)}, u32[]{:S(2)}, u32[]{:S(2)}) %collective-permute-start.3) | collective-permute-done | bytes 32800 | tf_op jit(solution)/shard_map/ppermute | solution.py:30
  11.3 0.5 %collective-permute-start.5 = (f32[64,256]{1,0:T(8,128)S(1)}, f32[64,256]{1,0:T(8,128)S(1)}, u32[]{:S(2)}, u32[]{:S(2)}) collective-permute-start(f32[64,256]{1,0:T(8,128)S(1)} %constant_dynamic-update-slice_fusion.own_cd), channel_id=1, source_target_pairs={{0,2},{1,3},{2,0},{3,1},{4,8},{5,9},{6,10},{7,11},{8,4},{9,5},{10,... | collective-permute-start | bytes 196616 | tf_op jit(solution)/shard_map/ppermute | solution.py:40
  11.8 1.2 %collective-permute-start.4 = (f32[64,256]{1,0:T(8,128)S(1)}, f32[64,256]{1,0:T(8,128)S(1)}, u32[]{:S(2)}, u32[]{:S(2)}) collective-permute-start(f32[64,256]{1,0:T(8,128)S(1)} %constant_dynamic-update-slice_fusion.own_cd), channel_id=1, source_target_pairs={{0,4},{4,0},{8,12},{12,8},{16,20},{20,16},{24,28},{28,24},{1,5},{5... | collective-permute-start | bytes 196616 | tf_op jit(solution)/shard_map/ppermute | solution.py:30
  13.0 2.6 %collective-permute-done.5.far_cd = f32[64,256]{1,0:T(8,128)S(1)} collective-permute-done((f32[64,256]{1,0:T(8,128)S(1)}, f32[64,256]{1,0:T(8,128)S(1)}, u32[]{:S(2)}, u32[]{:S(2)}) %collective-permute-start.5) | collective-permute-done | bytes 65568 | tf_op jit(solution)/shard_map/ppermute | solution.py:40
  15.6 0.0 collective-permute-done.4.near_cd
  15.6 0.0 collective-permute-done.1.far_ref
  15.6 0.0 collective-permute-done.near_ref
  15.6 2.4 %down.1 = (f32[13,3,112,128]{3,2,1,0:T(8,128)S(1)}, f32[13,3,64,128]{3,2,1,0:T(8,128)S(1)}, f32[13,3,40,128]{3,2,1,0:T(8,128)S(1)}, f32[288,128]{1,0:T(8,128)S(1)}) custom-call(f32[9,32,256]{2,1,0:T(8,128)S(1)} %get-tuple-element.9.own_ref, f32[9,32,256]{2,1,0:T(8,128)S(1)} %collective-permute-done.near_ref, ...), custom_call_target="tpu_custom_call" | custom-call | tf_op jit(solution)/shard_map/down/pallas_call | solution.py:494
  18.0 10.9 %all_to_all.5 = f32[32,1,1152]{2,1,0:T(1,128)S(1)} all-to-all(f32[32,1,1152]{2,1,0:T(1,128)S(1)} %bitcast.3), channel_id=1, replica_groups=mesh['gx'=8,'gy'=4] {'gx','gy'}, dimensions={0} | all-to-all | bytes 294912 | tf_op jit(solution)/shard_map/all_to_all | solution.py:503
  28.9 3.5 %up.1 = (f32[2,32,256]{2,1,0:T(8,128)}, f32[2,32,256]{2,1,0:T(8,128)}) custom-call(f32[288,128]{1,0:T(8,128)S(1)} %bitcast.2, f32[13,3,112,128]{3,2,1,0:T(8,128)S(1)} %get-tuple-element.13.l0, f32[13,3,64,128]{3,2,1,0:T(8,128)S(1)} %get-tuple-element.14.l1, f32[13,3,40,128]{3,2,1,0:T(8,128)S(1)} %get-tuple-element.15.l2), custom_call_target="tpu_custom_call" | custom-call | tf_op jit(solution)/shard_map/up/pallas_call | solution.py:509
  (2 shorter events, 0.0 us)
Async XLA Ops:
  1.8 6.2 %collective-permute-start.2 = (f32[32,256]{1,0:T(8,128)S(1)}, f32[32,256]{1,0:T(8,128)S(1)}, u32[]{:S(2)}, u32[]{:S(2)}) collective-permute-start(f32[32,256]{1,0:T(8,128)S(1)} %get-tuple-element.10), channel_id=1, source_target_pairs={{1,2},{2,1},{3,0},{0,3},{5,6},{6,5},{7,4},{4,7},{9,10},{10,9},{11,... | collective-permute-start | bytes 98312 | tf_op jit(solution)/shard_map/ppermute | solution.py:30
  5.7 9.9 %collective-permute-start.1 = (f32[9,32,256]{2,1,0:T(8,128)S(1)}, f32[9,32,256]{2,1,0:T(8,128)S(1)}, u32[]{:S(2)}, u32[]{:S(2)}) collective-permute-start(f32[9,32,256]{2,1,0:T(8,128)S(1)} %get-tuple-element.9.own_ref), channel_id=1, source_target_pairs={{0,2},{1,3},{2,0},{3,1},{4,8},{5,9},{6,10},{7,11},{8,4},{9,5},{10,... | collective-permute-start | bytes 884744 | tf_op jit(solution)/shard_map/ppermute | solution.py:40
  6.2 9.4 %collective-permute-start = (f32[9,32,256]{2,1,0:T(8,128)S(1)}, f32[9,32,256]{2,1,0:T(8,128)S(1)}, u32[]{:S(2)}, u32[]{:S(2)}) collective-permute-start(f32[9,32,256]{2,1,0:T(8,128)S(1)} %get-tuple-element.9.own_ref), channel_id=1, source_target_pairs={{0,4},{4,0},{8,12},{12,8},{16,20},{20,16},{24,28},{28,24},{1,5},{5... | collective-permute-start | bytes 884744 | tf_op jit(solution)/shard_map/ppermute | solution.py:30
  7.4 3.9 %collective-permute-start.3 = (f32[32,256]{1,0:T(8,128)S(1)}, f32[32,256]{1,0:T(8,128)S(1)}, u32[]{:S(2)}, u32[]{:S(2)}) collective-permute-start(f32[32,256]{1,0:T(8,128)S(1)} %get-tuple-element.11), channel_id=1, source_target_pairs={{0,1},{1,0},{2,3},{3,2},{4,5},{5,4},{6,7},{7,6},{8,9},{9,8},{10,11... | collective-permute-start | bytes 98312 | tf_op jit(solution)/shard_map/ppermute | solution.py:30
  11.3 4.3 %collective-permute-start.5 = (f32[64,256]{1,0:T(8,128)S(1)}, f32[64,256]{1,0:T(8,128)S(1)}, u32[]{:S(2)}, u32[]{:S(2)}) collective-permute-start(f32[64,256]{1,0:T(8,128)S(1)} %constant_dynamic-update-slice_fusion.own_cd), channel_id=1, source_target_pairs={{0,2},{1,3},{2,0},{3,1},{4,8},{5,9},{6,10},{7,11},{8,4},{9,5},{10,... | collective-permute-start | bytes 196616 | tf_op jit(solution)/shard_map/ppermute | solution.py:40
  11.8 3.8 %collective-permute-start.4 = (f32[64,256]{1,0:T(8,128)S(1)}, f32[64,256]{1,0:T(8,128)S(1)}, u32[]{:S(2)}, u32[]{:S(2)}) collective-permute-start(f32[64,256]{1,0:T(8,128)S(1)} %constant_dynamic-update-slice_fusion.own_cd), channel_id=1, source_target_pairs={{0,4},{4,0},{8,12},{12,8},{16,20},{20,16},{24,28},{28,24},{1,5},{5... | collective-permute-start | bytes 196616 | tf_op jit(solution)/shard_map/ppermute | solution.py:30

commit v6 on v5

--- a/solution.py
+++ b/solution.py
@@ -486,6 +486,8 @@
     far = far_permute(packed)
     near = pair_permute(packed, "gx", 0)
     strips = jnp.concatenate([strip_d, strip_c], axis=0)
+    nil = 0.0 * lax.axis_index("gy").astype(jnp.float32)
+    strips = lax.optimization_barrier(strips) + nil
     far_strips = far_permute(strips)
     near_strips = pair_permute(strips, "gx", 0)
 

time: 32.6 us -> 32.6 us (level)
  waiting for transfers between devices: 5.96 us -> 4.27 us
  blocking collectives: 10.9 us -> 12.5 us
    ppermute x4, waiting for transfers between devices: 3.38 us -> 1.69 us  [pair_permute(): return lax.ppermute(x, axis, pairs)]
    all_to_all x1, blocking collectives: 10.9 us -> 12.5 us  [on_device(): lax.all_to_all(pack.reshape(nx * ny, 1, PACK), ('gx', 'gy'), 0, 0, tiled=...]
    ppermute x4, starting transfers between devices: 6.87 us -> 7.26 us  [pair_permute(): return lax.ppermute(x, axis, pairs)]
    ppermute x2, starting transfers between devices: 1.01 us -> 0.68 us  [far_permute(): return lax.ppermute(x, ('gx', 'gy'), pairs)]
where the time goes in v6:
time: 32.6 us; the launch traced here: 32.4 us
  blocking collectives  12.5 us (38%)
  starting transfers between devices  7.94 us (24%)
  Pallas kernels  7.03 us (22%)
  waiting for transfers between devices  4.27 us (13%)
  between operations  0.66 us (2%)
    all_to_all x1, blocking collectives, on_device(): lax.all_to_all(pack.reshape(nx * ny, 1, PACK), ('gx', 'gy'), 0, 0, tiled=...  12.5 us
    ppermute x4, starting transfers between devices, pair_permute(): return lax.ppermute(x, axis, pairs)  7.26 us
    pallas_call x1, Pallas kernels, on_device(): pl.pallas_call(functools.partial(up_kernel, nx, ny), out_shape=(shape_of(...  3.48 us
    ppermute x2, waiting for transfers between devices, far_permute(): return lax.ppermute(x, ('gx', 'gy'), pairs)  2.58 us
    pallas_call x1, Pallas kernels, on_device(): pl.pallas_call(down_kernel, out_shape=tuple((shape_of(planes, 3, h, LANES...  2.43 us
    ppermute x4, waiting for transfers between devices, pair_permute(): return lax.ppermute(x, axis, pairs)  1.69 us
    pallas_call x1, Pallas kernels, on_device(): pl.pallas_call(pack_kernel, out_shape=(shape_of(PLANES, rows, cols),) + (...  1.12 us
    ppermute x2, starting transfers between devices, far_permute(): return lax.ppermute(x, ('gx', 'gy'), pairs)  0.68 us
  transfers between devices with their start and end apart: 6, of which 2 were waited for; matrix products, arithmetic and copies ran while one was open for 0% of the time, Pallas kernels for 0%

profile of v6, /device:TPU:0, one launch (start us, length us, event | category | flops | bytes accessed | tf_op | source)
XLA Modules:
  0.0 32.4 jit_solution(104565697496062011)
XLA Ops:
  0.6 1.1 %pack.1 = (f32[9,32,256]{2,1,0:T(8,128)S(1)}, f32[32,256]{1,0:T(8,128)S(1)}, f32[32,256]{1,0:T(8,128)S(1)}) custom-call(f32[2,32,256]{2,1,0:T(8,128)} %source.1, f32[2,32,256]{2,1,0:T(8,128)} %coef_x.1, f32[2,32,256]{2,1,0:T(8,128)} %coef_y.1, f32[2,32,256]{2,1,0:T(8,128)} %surface.1, f32[32,256]{1,0:T(8,128)} %coef_z.1), custom_call_target="tpu_custom_call" | custom-call | tf_op jit(solution)/shard_map/pack/pallas_call | solution.py:470
  1.8 4.0 %collective-permute-start.2 = (f32[32,256]{1,0:T(8,128)S(1)}, f32[32,256]{1,0:T(8,128)S(1)}, u32[]{:S(2)}, u32[]{:S(2)}) collective-permute-start(f32[32,256]{1,0:T(8,128)S(1)} %get-tuple-element.10), channel_id=1, source_target_pairs={{1,2},{2,1},{3,0},{0,3},{5,6},{6,5},{7,4},{4,7},{9,10},{10,9},{11,... | collective-permute-start | bytes 98312 | tf_op jit(solution)/shard_map/ppermute | solution.py:30
  5.7 0.5 %collective-permute-start.3 = (f32[32,256]{1,0:T(8,128)S(1)}, f32[32,256]{1,0:T(8,128)S(1)}, u32[]{:S(2)}, u32[]{:S(2)}) collective-permute-start(f32[32,256]{1,0:T(8,128)S(1)} %get-tuple-element.11), channel_id=1, source_target_pairs={{0,1},{1,0},{2,3},{3,2},{4,5},{5,4},{6,7},{7,6},{8,9},{9,8},{10,11... | collective-permute-start | bytes 98312 | tf_op jit(solution)/shard_map/ppermute | solution.py:30
  6.3 0.1 collective-permute-start.1
  6.4 1.6 %collective-permute-start = (f32[9,32,256]{2,1,0:T(8,128)S(1)}, f32[9,32,256]{2,1,0:T(8,128)S(1)}, u32[]{:S(2)}, u32[]{:S(2)}) collective-permute-start(f32[9,32,256]{2,1,0:T(8,128)S(1)} %get-tuple-element.9.own_ref), channel_id=1, source_target_pairs={{0,4},{4,0},{8,12},{12,8},{16,20},{20,16},{24,28},{28,24},{1,5},{5... | collective-permute-start | bytes 884744 | tf_op jit(solution)/shard_map/ppermute | solution.py:30
  7.9 0.0 collective-permute-done.2
  8.0 1.7 %collective-permute-done.3 = f32[32,256]{1,0:T(8,128)S(1)} collective-permute-done((f32[32,256]{1,0:T(8,128)S(1)}, f32[32,256]{1,0:T(8,128)S(1)}, u32[]{:S(2)}, u32[]{:S(2)}) %collective-permute-start.3) | collective-permute-done | bytes 32800 | tf_op jit(solution)/shard_map/ppermute | solution.py:30
  9.6 0.6 %collective-permute-start.5 = (f32[64,256]{1,0:T(8,128)S(1)}, f32[64,256]{1,0:T(8,128)S(1)}, u32[]{:S(2)}, u32[]{:S(2)}) collective-permute-start(f32[64,256]{1,0:T(8,128)S(1)} %broadcast_add_fusion.own_cd), channel_id=1, source_target_pairs={{0,2},{1,3},{2,0},{3,1},{4,8},{5,9},{6,10},{7,11},{8,4},{9,5},{10,... | collective-permute-start | bytes 196616 | tf_op jit(solution)/shard_map/ppermute | solution.py:40
  10.2 1.2 %collective-permute-start.4 = (f32[64,256]{1,0:T(8,128)S(1)}, f32[64,256]{1,0:T(8,128)S(1)}, u32[]{:S(2)}, u32[]{:S(2)}) collective-permute-start(f32[64,256]{1,0:T(8,128)S(1)} %broadcast_add_fusion.own_cd), channel_id=1, source_target_pairs={{0,4},{4,0},{8,12},{12,8},{16,20},{20,16},{24,28},{28,24},{1,5},{5... | collective-permute-start | bytes 196616 | tf_op jit(solution)/shard_map/ppermute | solution.py:30
  11.4 2.6 %collective-permute-done.5.far_cd = f32[64,256]{1,0:T(8,128)S(1)} collective-permute-done((f32[64,256]{1,0:T(8,128)S(1)}, f32[64,256]{1,0:T(8,128)S(1)}, u32[]{:S(2)}, u32[]{:S(2)}) %collective-permute-start.5) | collective-permute-done | bytes 65568 | tf_op jit(solution)/shard_map/ppermute | solution.py:40
  14.0 0.0 collective-permute-done.4.near_cd
  14.0 0.0 collective-permute-done.1.far_ref
  14.0 0.0 collective-permute-done.near_ref
  14.0 2.4 %down.1 = (f32[13,3,112,128]{3,2,1,0:T(8,128)S(1)}, f32[13,3,64,128]{3,2,1,0:T(8,128)S(1)}, f32[13,3,40,128]{3,2,1,0:T(8,128)S(1)}, f32[288,128]{1,0:T(8,128)S(1)}) custom-call(f32[9,32,256]{2,1,0:T(8,128)S(1)} %get-tuple-element.9.own_ref, f32[9,32,256]{2,1,0:T(8,128)S(1)} %collective-permute-done.near_ref, ...), custom_call_target="tpu_custom_call" | custom-call | tf_op jit(solution)/shard_map/down/pallas_call | solution.py:496
  16.4 12.5 %all_to_all.5 = f32[32,1,1152]{2,1,0:T(1,128)S(1)} all-to-all(f32[32,1,1152]{2,1,0:T(1,128)S(1)} %bitcast.3), channel_id=1, replica_groups=mesh['gx'=8,'gy'=4] {'gx','gy'}, dimensions={0} | all-to-all | bytes 294912 | tf_op jit(solution)/shard_map/all_to_all | solution.py:505
  28.9 3.5 %up.1 = (f32[2,32,256]{2,1,0:T(8,128)}, f32[2,32,256]{2,1,0:T(8,128)}) custom-call(f32[288,128]{1,0:T(8,128)S(1)} %bitcast.2, f32[13,3,112,128]{3,2,1,0:T(8,128)S(1)} %get-tuple-element.13.l0, f32[13,3,64,128]{3,2,1,0:T(8,128)S(1)} %get-tuple-element.14.l1, f32[13,3,40,128]{3,2,1,0:T(8,128)S(1)} %get-tuple-element.15.l2), custom_call_target="tpu_custom_call" | custom-call | tf_op jit(solution)/shard_map/up/pallas_call | solution.py:511
  (2 shorter events, 0.0 us)
Async XLA Ops:
  1.8 6.2 %collective-permute-start.2 = (f32[32,256]{1,0:T(8,128)S(1)}, f32[32,256]{1,0:T(8,128)S(1)}, u32[]{:S(2)}, u32[]{:S(2)}) collective-permute-start(f32[32,256]{1,0:T(8,128)S(1)} %get-tuple-element.10), channel_id=1, source_target_pairs={{1,2},{2,1},{3,0},{0,3},{5,6},{6,5},{7,4},{4,7},{9,10},{10,9},{11,... | collective-permute-start | bytes 98312 | tf_op jit(solution)/shard_map/ppermute | solution.py:30
  5.7 3.9 %collective-permute-start.3 = (f32[32,256]{1,0:T(8,128)S(1)}, f32[32,256]{1,0:T(8,128)S(1)}, u32[]{:S(2)}, u32[]{:S(2)}) collective-permute-start(f32[32,256]{1,0:T(8,128)S(1)} %get-tuple-element.11), channel_id=1, source_target_pairs={{0,1},{1,0},{2,3},{3,2},{4,5},{5,4},{6,7},{7,6},{8,9},{9,8},{10,11... | collective-permute-start | bytes 98312 | tf_op jit(solution)/shard_map/ppermute | solution.py:30
  6.3 7.7 %collective-permute-start.1 = (f32[9,32,256]{2,1,0:T(8,128)S(1)}, f32[9,32,256]{2,1,0:T(8,128)S(1)}, u32[]{:S(2)}, u32[]{:S(2)}) collective-permute-start(f32[9,32,256]{2,1,0:T(8,128)S(1)} %get-tuple-element.9.own_ref), channel_id=1, source_target_pairs={{0,2},{1,3},{2,0},{3,1},{4,8},{5,9},{6,10},{7,11},{8,4},{9,5},{10,... | collective-permute-start | bytes 884744 | tf_op jit(solution)/shard_map/ppermute | solution.py:40
  6.4 7.6 %collective-permute-start = (f32[9,32,256]{2,1,0:T(8,128)S(1)}, f32[9,32,256]{2,1,0:T(8,128)S(1)}, u32[]{:S(2)}, u32[]{:S(2)}) collective-permute-start(f32[9,32,256]{2,1,0:T(8,128)S(1)} %get-tuple-element.9.own_ref), channel_id=1, source_target_pairs={{0,4},{4,0},{8,12},{12,8},{16,20},{20,16},{24,28},{28,24},{1,5},{5... | collective-permute-start | bytes 884744 | tf_op jit(solution)/shard_map/ppermute | solution.py:30
  9.6 4.3 %collective-permute-start.5 = (f32[64,256]{1,0:T(8,128)S(1)}, f32[64,256]{1,0:T(8,128)S(1)}, u32[]{:S(2)}, u32[]{:S(2)}) collective-permute-start(f32[64,256]{1,0:T(8,128)S(1)} %broadcast_add_fusion.own_cd), channel_id=1, source_target_pairs={{0,2},{1,3},{2,0},{3,1},{4,8},{5,9},{6,10},{7,11},{8,4},{9,5},{10,... | collective-permute-start | bytes 196616 | tf_op jit(solution)/shard_map/ppermute | solution.py:40
  10.2 3.8 %collective-permute-start.4 = (f32[64,256]{1,0:T(8,128)S(1)}, f32[64,256]{1,0:T(8,128)S(1)}, u32[]{:S(2)}, u32[]{:S(2)}) collective-permute-start(f32[64,256]{1,0:T(8,128)S(1)} %broadcast_add_fusion.own_cd), channel_id=1, source_target_pairs={{0,4},{4,0},{8,12},{12,8},{16,20},{20,16},{24,28},{28,24},{1,5},{5... | collective-permute-start | bytes 196616 | tf_op jit(solution)/shard_map/ppermute | solution.py:30

commit v7 on v6

--- a/solution.py
+++ b/solution.py
@@ -287,17 +287,16 @@
     mine = place == (lane // 32 + lax.axis_index("gy")) % 4
     total = jnp.zeros((PLANES, LANES), jnp.float32)
     for r in range(4):
-        for c in range(2):
-            src = lax.broadcasted_iota(jnp.int32, (LANES, LANES), 0) + c * LANES
-            dst = lax.broadcasted_iota(jnp.int32, (LANES, LANES), 1)
-            group = (dst // 32 + lax.axis_index("gy")) % 4
-            pick = jnp.where((src == dst % 32 * 8) & (group == r), 1.0, 0.0)
-            total = total + jnp.dot(
-                nine[:, c, r, :],
-                pick,
-                precision=lax.Precision.HIGHEST,
-                preferred_element_type=jnp.float32,
-            )
+        src = lax.broadcasted_iota(jnp.int32, (2 * LANES, LANES), 0)
+        dst = lax.broadcasted_iota(jnp.int32, (2 * LANES, LANES), 1)
+        group = (dst // 32 + lax.axis_index("gy")) % 4
+        pick = jnp.where((src == dst % 32 * 8) & (group == r), 1.0, 0.0)
+        total = total + jnp.dot(
+            jnp.concatenate([nine[:, 0, r, :], nine[:, 1, r, :]], axis=1),
+            pick,
+            precision=lax.Precision.HIGHEST,
+            preferred_element_type=jnp.float32,
+        )
     row9[0:PLANES] = total
     row9[PLANES : 2 * PLANES] = total
     for r0 in range(0, pack_ref.shape[0], 8):

time: 32.6 us -> 32.4 us (level)
  no operation moved by 1% of the time
where the time goes in v7:
time: 32.4 us; the launch traced here: 32.2 us
  blocking collectives  12.5 us (39%)
  starting transfers between devices  7.94 us (25%)
  Pallas kernels  6.84 us (21%)
  waiting for transfers between devices  4.27 us (13%)
  between operations  0.66 us (2%)
    all_to_all x1, blocking collectives, on_device(): lax.all_to_all(pack.reshape(nx * ny, 1, PACK), ('gx', 'gy'), 0, 0, tiled=...  12.5 us
    ppermute x4, starting transfers between devices, pair_permute(): return lax.ppermute(x, axis, pairs)  7.26 us
    pallas_call x1, Pallas kernels, on_device(): pl.pallas_call(functools.partial(up_kernel, nx, ny), out_shape=(shape_of(...  3.48 us
    ppermute x2, waiting for transfers between devices, far_permute(): return lax.ppermute(x, ('gx', 'gy'), pairs)  2.58 us
    pallas_call x1, Pallas kernels, on_device(): pl.pallas_call(down_kernel, out_shape=tuple((shape_of(planes, 3, h, LANES...  2.24 us
    ppermute x4, waiting for transfers between devices, pair_permute(): return lax.ppermute(x, axis, pairs)  1.69 us
    pallas_call x1, Pallas kernels, on_device(): pl.pallas_call(pack_kernel, out_shape=(shape_of(PLANES, rows, cols),) + (...  1.12 us
    ppermute x2, starting transfers between devices, far_permute(): return lax.ppermute(x, ('gx', 'gy'), pairs)  0.68 us
  transfers between devices with their start and end apart: 6, of which 2 were waited for; matrix products, arithmetic and copies ran while one was open for 0% of the time, Pallas kernels for 0%

profile of v7, /device:TPU:0, one launch (start us, length us, event | category | flops | bytes accessed | tf_op | source)
XLA Modules:
  0.0 32.2 jit_solution(1772091689961697877)
XLA Ops:
  0.6 1.1 %pack.1 = (f32[9,32,256]{2,1,0:T(8,128)S(1)}, f32[32,256]{1,0:T(8,128)S(1)}, f32[32,256]{1,0:T(8,128)S(1)}) custom-call(f32[2,32,256]{2,1,0:T(8,128)} %source.1, f32[2,32,256]{2,1,0:T(8,128)} %coef_x.1, f32[2,32,256]{2,1,0:T(8,128)} %coef_y.1, f32[2,32,256]{2,1,0:T(8,128)} %surface.1, f32[32,256]{1,0:T(8,128)} %coef_z.1), custom_call_target="tpu_custom_call" | custom-call | tf_op jit(solution)/shard_map/pack/pallas_call | solution.py:469
  1.8 4.0 %collective-permute-start.2 = (f32[32,256]{1,0:T(8,128)S(1)}, f32[32,256]{1,0:T(8,128)S(1)}, u32[]{:S(2)}, u32[]{:S(2)}) collective-permute-start(f32[32,256]{1,0:T(8,128)S(1)} %get-tuple-element.10), channel_id=1, source_target_pairs={{1,2},{2,1},{3,0},{0,3},{5,6},{6,5},{7,4},{4,7},{9,10},{10,9},{11,... | collective-permute-start | bytes 98312 | tf_op jit(solution)/shard_map/ppermute | solution.py:30
  5.7 0.5 %collective-permute-start.3 = (f32[32,256]{1,0:T(8,128)S(1)}, f32[32,256]{1,0:T(8,128)S(1)}, u32[]{:S(2)}, u32[]{:S(2)}) collective-permute-start(f32[32,256]{1,0:T(8,128)S(1)} %get-tuple-element.11), channel_id=1, source_target_pairs={{0,1},{1,0},{2,3},{3,2},{4,5},{5,4},{6,7},{7,6},{8,9},{9,8},{10,11... | collective-permute-start | bytes 98312 | tf_op jit(solution)/shard_map/ppermute | solution.py:30
  6.3 0.1 collective-permute-start.1
  6.4 1.6 %collective-permute-start = (f32[9,32,256]{2,1,0:T(8,128)S(1)}, f32[9,32,256]{2,1,0:T(8,128)S(1)}, u32[]{:S(2)}, u32[]{:S(2)}) collective-permute-start(f32[9,32,256]{2,1,0:T(8,128)S(1)} %get-tuple-element.9.own_ref), channel_id=1, source_target_pairs={{0,4},{4,0},{8,12},{12,8},{16,20},{20,16},{24,28},{28,24},{1,5},{5... | collective-permute-start | bytes 884744 | tf_op jit(solution)/shard_map/ppermute | solution.py:30
  7.9 0.0 collective-permute-done.2
  8.0 1.7 %collective-permute-done.3 = f32[32,256]{1,0:T(8,128)S(1)} collective-permute-done((f32[32,256]{1,0:T(8,128)S(1)}, f32[32,256]{1,0:T(8,128)S(1)}, u32[]{:S(2)}, u32[]{:S(2)}) %collective-permute-start.3) | collective-permute-done | bytes 32800 | tf_op jit(solution)/shard_map/ppermute | solution.py:30
  9.6 0.6 %collective-permute-start.5 = (f32[64,256]{1,0:T(8,128)S(1)}, f32[64,256]{1,0:T(8,128)S(1)}, u32[]{:S(2)}, u32[]{:S(2)}) collective-permute-start(f32[64,256]{1,0:T(8,128)S(1)} %broadcast_add_fusion.own_cd), channel_id=1, source_target_pairs={{0,2},{1,3},{2,0},{3,1},{4,8},{5,9},{6,10},{7,11},{8,4},{9,5},{10,... | collective-permute-start | bytes 196616 | tf_op jit(solution)/shard_map/ppermute | solution.py:40
  10.2 1.2 %collective-permute-start.4 = (f32[64,256]{1,0:T(8,128)S(1)}, f32[64,256]{1,0:T(8,128)S(1)}, u32[]{:S(2)}, u32[]{:S(2)}) collective-permute-start(f32[64,256]{1,0:T(8,128)S(1)} %broadcast_add_fusion.own_cd), channel_id=1, source_target_pairs={{0,4},{4,0},{8,12},{12,8},{16,20},{20,16},{24,28},{28,24},{1,5},{5... | collective-permute-start | bytes 196616 | tf_op jit(solution)/shard_map/ppermute | solution.py:30
  11.4 2.6 %collective-permute-done.5.far_cd = f32[64,256]{1,0:T(8,128)S(1)} collective-permute-done((f32[64,256]{1,0:T(8,128)S(1)}, f32[64,256]{1,0:T(8,128)S(1)}, u32[]{:S(2)}, u32[]{:S(2)}) %collective-permute-start.5) | collective-permute-done | bytes 65568 | tf_op jit(solution)/shard_map/ppermute | solution.py:40
  14.0 0.0 collective-permute-done.4.near_cd
  14.0 0.0 collective-permute-done.1.far_ref
  14.0 0.0 collective-permute-done.near_ref
  14.0 2.2 %down.1 = (f32[13,3,112,128]{3,2,1,0:T(8,128)S(1)}, f32[13,3,64,128]{3,2,1,0:T(8,128)S(1)}, f32[13,3,40,128]{3,2,1,0:T(8,128)S(1)}, f32[288,128]{1,0:T(8,128)S(1)}) custom-call(f32[9,32,256]{2,1,0:T(8,128)S(1)} %get-tuple-element.9.own_ref, f32[9,32,256]{2,1,0:T(8,128)S(1)} %collective-permute-done.near_ref, ...), custom_call_target="tpu_custom_call" | custom-call | tf_op jit(solution)/shard_map/down/pallas_call | solution.py:495
  16.2 12.5 %all_to_all.5 = f32[32,1,1152]{2,1,0:T(1,128)S(1)} all-to-all(f32[32,1,1152]{2,1,0:T(1,128)S(1)} %bitcast.3), channel_id=1, replica_groups=mesh['gx'=8,'gy'=4] {'gx','gy'}, dimensions={0} | all-to-all | bytes 294912 | tf_op jit(solution)/shard_map/all_to_all | solution.py:504
  28.7 3.5 %up.1 = (f32[2,32,256]{2,1,0:T(8,128)}, f32[2,32,256]{2,1,0:T(8,128)}) custom-call(f32[288,128]{1,0:T(8,128)S(1)} %bitcast.2, f32[13,3,112,128]{3,2,1,0:T(8,128)S(1)} %get-tuple-element.13.l0, f32[13,3,64,128]{3,2,1,0:T(8,128)S(1)} %get-tuple-element.14.l1, f32[13,3,40,128]{3,2,1,0:T(8,128)S(1)} %get-tuple-element.15.l2), custom_call_target="tpu_custom_call" | custom-call | tf_op jit(solution)/shard_map/up/pallas_call | solution.py:510
  (2 shorter events, 0.0 us)
Async XLA Ops:
  1.8 6.2 %collective-permute-start.2 = (f32[32,256]{1,0:T(8,128)S(1)}, f32[32,256]{1,0:T(8,128)S(1)}, u32[]{:S(2)}, u32[]{:S(2)}) collective-permute-start(f32[32,256]{1,0:T(8,128)S(1)} %get-tuple-element.10), channel_id=1, source_target_pairs={{1,2},{2,1},{3,0},{0,3},{5,6},{6,5},{7,4},{4,7},{9,10},{10,9},{11,... | collective-permute-start | bytes 98312 | tf_op jit(solution)/shard_map/ppermute | solution.py:30
  5.7 3.9 %collective-permute-start.3 = (f32[32,256]{1,0:T(8,128)S(1)}, f32[32,256]{1,0:T(8,128)S(1)}, u32[]{:S(2)}, u32[]{:S(2)}) collective-permute-start(f32[32,256]{1,0:T(8,128)S(1)} %get-tuple-element.11), channel_id=1, source_target_pairs={{0,1},{1,0},{2,3},{3,2},{4,5},{5,4},{6,7},{7,6},{8,9},{9,8},{10,11... | collective-permute-start | bytes 98312 | tf_op jit(solution)/shard_map/ppermute | solution.py:30
  6.3 7.7 %collective-permute-start.1 = (f32[9,32,256]{2,1,0:T(8,128)S(1)}, f32[9,32,256]{2,1,0:T(8,128)S(1)}, u32[]{:S(2)}, u32[]{:S(2)}) collective-permute-start(f32[9,32,256]{2,1,0:T(8,128)S(1)} %get-tuple-element.9.own_ref), channel_id=1, source_target_pairs={{0,2},{1,3},{2,0},{3,1},{4,8},{5,9},{6,10},{7,11},{8,4},{9,5},{10,... | collective-permute-start | bytes 884744 | tf_op jit(solution)/shard_map/ppermute | solution.py:40
  6.4 7.6 %collective-permute-start = (f32[9,32,256]{2,1,0:T(8,128)S(1)}, f32[9,32,256]{2,1,0:T(8,128)S(1)}, u32[]{:S(2)}, u32[]{:S(2)}) collective-permute-start(f32[9,32,256]{2,1,0:T(8,128)S(1)} %get-tuple-element.9.own_ref), channel_id=1, source_target_pairs={{0,4},{4,0},{8,12},{12,8},{16,20},{20,16},{24,28},{28,24},{1,5},{5... | collective-permute-start | bytes 884744 | tf_op jit(solution)/shard_map/ppermute | solution.py:30
  9.6 4.3 %collective-permute-start.5 = (f32[64,256]{1,0:T(8,128)S(1)}, f32[64,256]{1,0:T(8,128)S(1)}, u32[]{:S(2)}, u32[]{:S(2)}) collective-permute-start(f32[64,256]{1,0:T(8,128)S(1)} %broadcast_add_fusion.own_cd), channel_id=1, source_target_pairs={{0,2},{1,3},{2,0},{3,1},{4,8},{5,9},{6,10},{7,11},{8,4},{9,5},{10,... | collective-permute-start | bytes 196616 | tf_op jit(solution)/shard_map/ppermute | solution.py:40
  10.2 3.8 %collective-permute-start.4 = (f32[64,256]{1,0:T(8,128)S(1)}, f32[64,256]{1,0:T(8,128)S(1)}, u32[]{:S(2)}, u32[]{:S(2)}) collective-permute-start(f32[64,256]{1,0:T(8,128)S(1)} %broadcast_add_fusion.own_cd), channel_id=1, source_target_pairs={{0,4},{4,0},{8,12},{12,8},{16,20},{20,16},{24,28},{28,24},{1,5},{5... | collective-permute-start | bytes 196616 | tf_op jit(solution)/shard_map/ppermute | solution.py:30
